TPU v7x, 32 devices: a whole 2x2x4 slice. The times are simulated.
32 devices in a mesh: section: 4 (over y, x), dp: 8 (over z, core).
Axes of the slice: x: 2, y: 2, z: 4, core: 2. Of those that a mesh axis runs over, the one named last changes fastest.
Arguments:
- patches: bfloat16 [2, 8, 256, 768], P(None, 'dp'), may hold values from -6 to 6
- lengths: int32 [2, 8], P(None, 'dp'), may hold values from 51 to 256, as said below
- qkv_weight: bfloat16 [4, 768, 2304], P('section'), may hold values from -0.21875 to 0.21875
- out_weight: bfloat16 [4, 768, 768], P('section'), may hold values from -1.75 to 1.75
- up_weight: bfloat16 [4, 768, 3072], P('section'), may hold values from -0.21875 to 0.21875
- down_weight: bfloat16 [4, 3072, 768], P('section'), may hold values from -0.109375 to 0.109375
- vectors: float32 [4, 9216], P('section'), may hold values from -1.5 to 1.5
- cotangent: bfloat16 [2, 8, 256, 768], P(None, 'dp'), may hold values from -6 to 6
Outputs:
- layer_outputs: bfloat16 [4, 2, 8, 256, 768], P('section', None, 'dp')
- input_grads: float32 [4, 2, 8, 256, 768], P('section', None, 'dp')
- qkv_grad: float32 [4, 768, 2304], P('section', 'dp')
- out_grad: float32 [4, 768, 768], P('section', 'dp')
- up_grad: float32 [4, 768, 3072], P('section', 'dp')
- down_grad: float32 [4, 3072, 768], P('section', 'dp')
- vector_grad: float32 [4, 9216], P('section', 'dp')
Inputs may be any that keep to these rules, and one draw needn't show every extreme that they name: `lengths`: patches of a clip at positions from its length on are padding; some clip in every draw has exactly 256 valid patches.
All inputs are finite; a program needn't handle non-finite values.
Results may differ from a plain program's by a relative error of at most 0.012.
Values may be sent and summed in bfloat16 or wider, within the bound.
A program may use at most 512 MiB of HBM per device.

v0:
```python
from functools import partial
import math

import jax
import jax.numpy as jnp
from jax import lax
from jax.sharding import PartitionSpec as P

HEADS = 12
HEAD_DIM = 64


EPS = 1e-06


def shifted(x, axis, by):
    peers = lax.axis_size(axis)
    pairs = [(i, i + by) for i in range(peers) if 0 <= i + by < peers]
    return lax.ppermute(x, axis, pairs)


def matmul(left, right):
    return jnp.dot(left, right, preferred_element_type=jnp.float32)


def normalize(hidden):
    average = jnp.mean(hidden, axis=-1, keepdims=True)
    centered = hidden - average
    inverse = lax.rsqrt(jnp.mean(centered * centered, axis=-1, keepdims=True) + EPS)
    return (centered * inverse, inverse)


def norm_back(grad, unit, inverse):
    return inverse * (
        grad
        - jnp.mean(grad, axis=-1, keepdims=True)
        - unit * jnp.mean(grad * unit, axis=-1, keepdims=True)
    )


def split_vector(vector, feature_width):
    pieces = [
        vector[piece_index * feature_width : (piece_index + 1) * feature_width]
        for piece_index in range(8)
    ]
    return pieces + [vector[8 * feature_width :]]


def forward_parts(block_in, key_valid, weights, vector):
    qkv_weight, out_weight, up_weight, down_weight = weights
    row_count, feature_width = block_in.shape
    gain_one, shift_one, bias_q, bias_v, bias_o, gain_two, shift_two, bias_d, bias_u = split_vector(
        vector, feature_width
    )
    residual = block_in.astype(jnp.float32)
    unit_one, inverse_one = normalize(residual)
    normed_one = (unit_one * (1.0 + gain_one) + shift_one).astype(jnp.bfloat16)
    projected = matmul(normed_one, qkv_weight)
    queries = (
        (projected[:, :feature_width] + bias_q)
        .astype(jnp.bfloat16)
        .reshape(row_count, HEADS, HEAD_DIM)
    )
    key_heads = (
        projected[:, feature_width : 2 * feature_width]
        .astype(jnp.bfloat16)
        .reshape(row_count, HEADS, HEAD_DIM)
    )
    value_heads = (
        (projected[:, 2 * feature_width :] + bias_v)
        .astype(jnp.bfloat16)
        .reshape(row_count, HEADS, HEAD_DIM)
    )
    score_scale = 1.0 / math.sqrt(HEAD_DIM)
    scores = (
        jnp.einsum("qhd,khd->hqk", queries, key_heads, preferred_element_type=jnp.float32)
        * score_scale
    )
    scores = jnp.where(key_valid[None, None, :], scores, -1e30)
    soft_weights = jax.nn.softmax(scores, axis=-1)
    weights_low = soft_weights.astype(jnp.bfloat16)
    attended = (
        jnp.einsum("hqk,khd->qhd", weights_low, value_heads, preferred_element_type=jnp.float32)
        .reshape(row_count, feature_width)
        .astype(jnp.bfloat16)
    )
    residual_one = residual + (matmul(attended, out_weight) + bias_o)
    unit_two, inverse_two = normalize(residual_one)
    normed_two = (unit_two * (1.0 + gain_two) + shift_two).astype(jnp.bfloat16)
    upward = matmul(normed_two, up_weight) + bias_u
    activated = jax.nn.gelu(upward, approximate=False).astype(jnp.bfloat16)
    result = residual_one + (matmul(activated, down_weight) + bias_d)
    saved = (
        unit_one,
        inverse_one,
        normed_one,
        queries,
        key_heads,
        value_heads,
        soft_weights,
        weights_low,
        attended,
        unit_two,
        inverse_two,
        normed_two,
        upward,
        activated,
    )
    return (result, saved)


def backward_parts(block_in, key_valid, weights, vector, grad_out):
    qkv_weight, out_weight, up_weight, down_weight = weights
    row_count, feature_width = block_in.shape
    gain_one, shift_one, bias_q, bias_v, bias_o, gain_two, shift_two, bias_d, bias_u = split_vector(
        vector, feature_width
    )
    result, saved = forward_parts(block_in, key_valid, weights, vector)
    (
        unit_one,
        inverse_one,
        normed_one,
        queries,
        key_heads,
        value_heads,
        soft_weights,
        weights_low,
        attended,
        unit_two,
        inverse_two,
        normed_two,
        upward,
        activated,
    ) = saved
    score_scale = 1.0 / math.sqrt(HEAD_DIM)
    grad_down = grad_out.astype(jnp.bfloat16)
    down_grad = matmul(activated.T, grad_down)
    grad_bias_d = jnp.sum(grad_down.astype(jnp.float32), axis=0)
    grad_act = matmul(grad_down, down_weight.T)
    gelu_pull = jax.vjp(partial(jax.nn.gelu, approximate=False), upward)[1]
    grad_up = gelu_pull(grad_act)[0].astype(jnp.bfloat16)
    up_grad = matmul(normed_two.T, grad_up)
    grad_bias_u = jnp.sum(grad_up.astype(jnp.float32), axis=0)
    grad_two = matmul(grad_up, up_weight.T)
    grad_gain_two = jnp.sum(grad_two * unit_two, axis=0)
    grad_shift_two = jnp.sum(grad_two, axis=0)
    grad_mid = grad_out + norm_back(grad_two * (1.0 + gain_two), unit_two, inverse_two)
    grad_branch = grad_mid.astype(jnp.bfloat16)
    out_grad = matmul(attended.T, grad_branch)
    grad_bias_o = jnp.sum(grad_branch.astype(jnp.float32), axis=0)
    grad_att = (
        matmul(grad_branch, out_weight.T).astype(jnp.bfloat16).reshape(row_count, HEADS, HEAD_DIM)
    )
    grad_soft = jnp.einsum(
        "qhd,khd->hqk", grad_att, value_heads, preferred_element_type=jnp.float32
    )
    grad_values = jnp.einsum(
        "hqk,qhd->khd", weights_low, grad_att, preferred_element_type=jnp.float32
    )
    inner_sum = jnp.sum(grad_soft * soft_weights, axis=-1, keepdims=True)
    grad_scores = (soft_weights * (grad_soft - inner_sum)).astype(jnp.bfloat16)
    grad_queries = (
        jnp.einsum("hqk,khd->qhd", grad_scores, key_heads, preferred_element_type=jnp.float32)
        * score_scale
    )
    grad_keys = (
        jnp.einsum("hqk,qhd->khd", grad_scores, queries, preferred_element_type=jnp.float32)
        * score_scale
    )
    grad_projected = jnp.concatenate(
        (
            grad_queries.reshape(row_count, feature_width),
            grad_keys.reshape(row_count, feature_width),
            grad_values.reshape(row_count, feature_width),
        ),
        axis=1,
    ).astype(jnp.bfloat16)
    qkv_grad = matmul(normed_one.T, grad_projected)
    grad_bias_q = jnp.sum(grad_projected[:, :feature_width].astype(jnp.float32), axis=0)
    grad_bias_v = jnp.sum(grad_projected[:, 2 * feature_width :].astype(jnp.float32), axis=0)
    grad_one = matmul(grad_projected, qkv_weight.T)
    grad_gain_one = jnp.sum(grad_one * unit_one, axis=0)
    grad_shift_one = jnp.sum(grad_one, axis=0)
    grad_in = grad_mid + norm_back(grad_one * (1.0 + gain_one), unit_one, inverse_one)
    vector_grad = jnp.concatenate(
        (
            grad_gain_one,
            grad_shift_one,
            grad_bias_q,
            grad_bias_v,
            grad_bias_o,
            grad_gain_two,
            grad_shift_two,
            grad_bias_d,
            grad_bias_u,
        )
    )
    return ((qkv_grad, out_grad, up_grad, down_grad, vector_grad), grad_in)


def shards(patches, lengths, qkv_weight, out_weight, up_weight, down_weight, vectors, cotangent):
    section_index = lax.axis_index("section")
    section_count = lax.axis_size("section")
    micro_count = patches.shape[0]
    row_count = patches.shape[2]
    feature_width = patches.shape[3]
    weights = (qkv_weight[0], out_weight[0], up_weight[0], down_weight[0])
    vector = vectors[0]
    positions = jnp.arange(row_count, dtype=jnp.int32)
    fresh_inputs = patches[:, 0]
    targets = cotangent[:, 0]
    clip_lengths = lengths[:, 0]
    stored = jnp.zeros((micro_count, row_count, feature_width), jnp.bfloat16)
    produced = jnp.zeros((micro_count, row_count, feature_width), jnp.bfloat16)
    arrived = jnp.zeros((row_count, feature_width), jnp.bfloat16)
    step_count = micro_count + section_count - 1
    for moment in range(step_count):
        offset = moment - section_index
        active = (offset >= 0) & (offset < micro_count)
        slot_index = jnp.clip(offset, 0, micro_count - 1)
        incoming = lax.dynamic_index_in_dim(fresh_inputs, slot_index, 0, keepdims=False)
        block_in = jnp.where(section_index == 0, incoming, arrived)
        key_valid = positions < lax.dynamic_index_in_dim(
            clip_lengths, slot_index, 0, keepdims=False
        )
        result = lax.cond(
            active,
            lambda: forward_parts(block_in, key_valid, weights, vector)[0].astype(jnp.bfloat16),
            lambda: jnp.zeros((row_count, feature_width), jnp.bfloat16),
        )
        stored = jnp.where(
            active, lax.dynamic_update_index_in_dim(stored, block_in, slot_index, 0), stored
        )
        produced = jnp.where(
            active, lax.dynamic_update_index_in_dim(produced, result, slot_index, 0), produced
        )
        if moment + 1 < step_count:
            arrived = shifted(result, "section", 1)
    zero_grads = (
        jnp.zeros(weights[0].shape, jnp.float32),
        jnp.zeros(weights[1].shape, jnp.float32),
        jnp.zeros(weights[2].shape, jnp.float32),
        jnp.zeros(weights[3].shape, jnp.float32),
        jnp.zeros(vector.shape, jnp.float32),
    )
    totals = zero_grads
    input_grads = jnp.zeros((micro_count, row_count, feature_width), jnp.float32)
    returned = jnp.zeros((row_count, feature_width), jnp.bfloat16)
    for moment in range(step_count):
        offset = moment - (section_count - 1 - section_index)
        active = (offset >= 0) & (offset < micro_count)
        slot_index = jnp.clip(offset, 0, micro_count - 1)
        key_valid = positions < lax.dynamic_index_in_dim(
            clip_lengths, slot_index, 0, keepdims=False
        )
        target = lax.dynamic_index_in_dim(targets, slot_index, 0, keepdims=False).astype(
            jnp.float32
        )
        target = jnp.where(key_valid[:, None], target, 0.0)
        grad_out = jnp.where(
            section_index == section_count - 1, target, returned.astype(jnp.float32)
        )
        block_in = lax.dynamic_index_in_dim(stored, slot_index, 0, keepdims=False)
        gradients, grad_in = lax.cond(
            active,
            lambda: backward_parts(block_in, key_valid, weights, vector, grad_out),
            lambda: (zero_grads, jnp.zeros((row_count, feature_width), jnp.float32)),
        )
        input_grads = jnp.where(
            active,
            lax.dynamic_update_index_in_dim(input_grads, grad_in, slot_index, 0),
            input_grads,
        )
        totals = jax.tree.map(jnp.add, totals, gradients)
        if moment + 1 < step_count:
            returned = shifted(grad_in.astype(jnp.bfloat16), "section", -1)
    collected = (
        lax.psum_scatter(totals[0][None], "dp", scatter_dimension=1, tiled=True),
        lax.psum_scatter(totals[1][None], "dp", scatter_dimension=1, tiled=True),
        lax.psum_scatter(totals[2][None], "dp", scatter_dimension=1, tiled=True),
        lax.psum_scatter(totals[3][None], "dp", scatter_dimension=1, tiled=True),
        lax.psum_scatter(totals[4][None], "dp", scatter_dimension=1, tiled=True),
    )
    return (
        produced[None, :, None],
        input_grads[None, :, None],
        collected[0],
        collected[1],
        collected[2],
        collected[3],
        collected[4],
    )


def solution(mesh):
    placed = (
        P(None, "dp", None, None),
        P(None, "dp"),
        P("section", None, None),
        P("section", None, None),
        P("section", None, None),
        P("section", None, None),
        P("section", None),
        P(None, "dp", None, None),
    )
    return jax.shard_map(
        shards,
        mesh=mesh,
        in_specs=placed,
        out_specs=(
            P("section", None, "dp", None, None),
            P("section", None, "dp", None, None),
            P("section", "dp", None),
            P("section", "dp", None),
            P("section", "dp", None),
            P("section", "dp", None),
            P("section", "dp"),
        ),
        check_vma=False,
    )
```

profile of v0, /device:TPU:0, one launch (start us, length us, event | category | flops | bytes accessed | tf_op | source)
XLA Modules:
  0.0 991.5 jit_solution(8706807335364962936)
XLA Ops:
  8.3 29.0 %conditional.10 = (bf16[256,768]{1,0:T(8,128)(2,1)}, bf16[1,256,768]{2,1,0:T(8,128)(2,1)S(1)}) conditional(s32[]{:T(128)} %convert_element_type.1056, () %tuple.154, (bf16[1,1,256,768]{3,2,1,0:T(8,128)(2,1)S(1)}, pred[256,768]{1,0:T(32,128)(4,1)S(1)}, f32[9216]{0:T(1024)}, bf16[768,2304]{1,0:T(8,128)(2,1)}, s32[2,1]{0,1:T(1,128)}, ...), branch_computations={%region_0.1_spmd, %region_1.8_spmd} | conditional | flops 3888908800 | bytes 41049660 | solution.py:226
  12.3 3.2 fusion.37
  16.3 2.9 fusion.732
  19.1 2.4 fusion.25
  22.4 13.6 %fusion.26 = bf16[256,768]{1,0:T(8,128)(2,1)} fusion(f32[256,768]{1,0:T(8,128)S(1)} %get-tuple-element.1355, bf16[3072,768]{1,0:T(8,128)(2,1)} %get-tuple-element.1088, f32[3072]{0:T(1024)S(1)} %slice.590, bf16[768,3072]{1,0:T(8,128)(2,1)} %get-tuple-element.1087, f32[768]{0:T(1024)S(1)} %get-tuple-element.1345, f32[768]{0:T(1024)S(1)} %get-tuple-element.1346, ...), kind=kOutput, calls=%fused_computation.35 | convolution fusion | flops 2469396480 | bytes 10640384 | tf_op jit(solution)/shard_map/cond/branch_1_fun/dot_general | solution.py:23
  39.7 8.6 collective-permute-done
  48.6 35.6 %conditional.11 = (bf16[256,768]{1,0:T(8,128)(2,1)}, bf16[1,256,768]{2,1,0:T(8,128)(2,1)S(1)}) conditional(s32[]{:T(128)} %convert_element_type.1057, () %tuple.156, (bf16[256,768]{1,0:T(8,128)(2,1)S(1)}, f32[9216]{0:T(1024)S(1)}, bf16[768,2304]{1,0:T(8,128)(2,1)}, s32[2,1]{0,1:T(1,128)S(1)}, s32[]{:T(128)}, /*index=5*/s32[256]{0:T(256)S(1)}, ...), branch_computations={%region_8.9_spmd, %region_9.16_spmd} | conditional | flops 3888122368 | bytes 38690364 | solution.py:226
  50.3 3.2 fusion.122
  61.0 4.0 fusion.734
  64.9 2.4 fusion.110
  69.1 14.0 %fusion.111 = bf16[256,768]{1,0:T(8,128)(2,1)} fusion(f32[256,768]{1,0:T(8,128)} %copy-done.41, bf16[3072,768]{1,0:T(8,128)(2,1)} %get-tuple-element.1097, f32[3072]{0:T(1024)S(1)} %slice.602, bf16[768,3072]{1,0:T(8,128)(2,1)} %get-tuple-element.1096, f32[768]{0:T(1024)S(1)} %get-tuple-element.1359, f32[768]{0:T(1024)S(1)} %get-tuple-element.1360, ...), kind=kOutput, calls=%fused_computation.137 | convolution fusion | flops 2469396480 | bytes 10640384 | tf_op jit(solution)/shard_map/cond/branch_1_fun/dot_general | solution.py:23
  84.2 6.1 collective-permute-start.1
  90.3 8.0 collective-permute-done.1
  99.7 40.8 %collective-permute-start.2 = (bf16[256,768]{1,0:T(8,128)(2,1)}, bf16[256,768]{1,0:T(8,128)(2,1)}, u32[]{:S(2)}, u32[]{:S(2)}) collective-permute-start(bf16[256,768]{1,0:T(8,128)(2,1)} %get-tuple-element.1243), channel_id=1, source_target_pairs={{0,8},{8,16},{16,24},{1,9},{9,17},{17,25},{2,10},{10,18},{18,26},{... | collective-permute-start | bytes 1179656 | tf_op jit(solution)/shard_map/ppermute | solution.py:19
  140.5 7.1 collective-permute-done.2
  148.8 6.1 collective-permute-start.3
  154.9 6.2 collective-permute-done.3
  162.8 20.2 %conditional.15 = (f32[768,2304]{1,0:T(8,128)}, f32[768,768]{1,0:T(8,128)}, f32[768,3072]{1,0:T(8,128)}, f32[3072,768]{1,0:T(8,128)}, f32[9216]{0:T(1024)S(1)}, /*index=5*/f32[256,768]{1,0:T(8,128)S(1)}) conditional(s32[]{:T(128)} %convert_element_type.1061, () %tuple.164, (bf16[2,256,768]{2,1,0:T(8,128)(2,1)S(1)}, s32[]{:T(128)}, ...), branch_computations={%region_40.41_spmd, %region_41.62_spmd} | conditional | flops 10371651584 | bytes 281237056 | solution.py:264
  164.5 3.3 broadcast_in_dim.544
  167.8 4.2 broadcast_in_dim.547
  172.0 4.8 broadcast_in_dim.546
  185.3 45.7 %collective-permute-done.4 = bf16[256,768]{1,0:T(8,128)(2,1)S(1)} collective-permute-done((bf16[256,768]{1,0:T(8,128)(2,1)S(1)}, bf16[256,768]{1,0:T(8,128)(2,1)S(1)}, u32[]{:S(2)}, u32[]{:S(2)}) %collective-permute-start.4) | collective-permute-done | bytes 393248 | tf_op jit(solution)/shard_map/ppermute | solution.py:19
  231.2 19.9 %conditional.16 = (f32[768,2304]{1,0:T(8,128)}, f32[768,768]{1,0:T(8,128)}, f32[768,3072]{1,0:T(8,128)}, f32[3072,768]{1,0:T(8,128)}, f32[9216]{0:T(1024)S(1)}, /*index=5*/f32[256,768]{1,0:T(8,128)S(1)}) conditional(s32[]{:T(128)} %convert_element_type.1062, () %tuple.166, (bf16[2,256,768]{2,1,0:T(8,128)(2,1)S(1)}, s32[]{:T(128)}, ...), branch_computations={%region_62.63_spmd, %region_63.84_spmd} | conditional | flops 10416083968 | bytes 249394512 | solution.py:264
  232.8 3.3 broadcast_in_dim.554
  236.1 4.2 broadcast_in_dim.557
  240.4 4.7 broadcast_in_dim.556
  253.4 10.1 %collective-permute-done.5 = bf16[256,768]{1,0:T(8,128)(2,1)S(1)} collective-permute-done((bf16[256,768]{1,0:T(8,128)(2,1)S(1)}, bf16[256,768]{1,0:T(8,128)(2,1)S(1)}, u32[]{:S(2)}, u32[]{:S(2)}) %collective-permute-start.5) | collective-permute-done | bytes 393248 | tf_op jit(solution)/shard_map/ppermute | solution.py:19
  263.5 20.2 %conditional.17 = (f32[768,2304]{1,0:T(8,128)}, f32[768,768]{1,0:T(8,128)}, f32[768,3072]{1,0:T(8,128)}, f32[3072,768]{1,0:T(8,128)}, f32[9216]{0:T(1024)S(1)}, /*index=5*/f32[256,768]{1,0:T(8,128)S(1)}) conditional(s32[]{:T(128)} %convert_element_type.1065, () %tuple.168, (bf16[2,256,768]{2,1,0:T(8,128)(2,1)S(1)}, s32[]{:T(128)}, ...), branch_computations={%region_84.85_spmd, %region_85.106_spmd} | conditional | flops 10416083968 | bytes 249562448 | solution.py:264
  265.2 3.4 broadcast_in_dim.563
  268.6 4.3 broadcast_in_dim.566
  272.9 4.7 broadcast_in_dim.565
  286.0 159.4 %collective-permute-done.6 = bf16[256,768]{1,0:T(8,128)(2,1)S(1)} collective-permute-done((bf16[256,768]{1,0:T(8,128)(2,1)S(1)}, bf16[256,768]{1,0:T(8,128)(2,1)S(1)}, u32[]{:S(2)}, u32[]{:S(2)}) %collective-permute-start.6) | collective-permute-done | bytes 393248 | tf_op jit(solution)/shard_map/ppermute | solution.py:19
  445.5 78.0 %conditional.18 = (f32[768,2304]{1,0:T(8,128)}, f32[768,768]{1,0:T(8,128)}, f32[768,3072]{1,0:T(8,128)}, f32[3072,768]{1,0:T(8,128)}, f32[9216]{0:T(1024)S(1)}, /*index=5*/f32[256,768]{1,0:T(8,128)S(1)}) conditional(s32[]{:T(128)} %convert_element_type.1068, () %tuple.170, (bf16[2,256,768]{2,1,0:T(8,128)(2,1)S(1)}, s32[]{:T(128)}, ...), branch_computations={%region_106.107_spmd, %region_107.128_spmd} | conditional | flops 10416083968 | bytes 249562448 | solution.py:264
  452.6 3.2 fusion.657
  463.4 4.6 fusion.748
  467.9 2.3 convolution_convert_fusion.11
  471.9 4.2 convolution_add_fusion.16
  476.2 9.9 %convert_reduce_fusion.23 = (f32[3072]{0:T(1024)}, bf16[256,3072]{1,0:T(8,128)(2,1)S(1)}) fusion(f32[256,3072]{1,0:T(8,128)S(1)} %convolution_add_fusion.16, bf16[3072,768]{1,0:T(8,128)(2,1)S(1)} %bitcast.766, f32[256,768]{1,0:T(8,128)S(1)} %get-tuple-element.1327), kind=kOutput, calls=%fused_computation.861 | convolution fusion | flops 1266349056 | bytes 10235904 | tf_op jit(solution)/shard_map/cond/branch_1_fun/dot_general | solution.py:23
  492.5 2.6 convolution_convert_fusion.9
  503.8 4.1 fusion.640
  508.0 9.9 fusion.611
  517.9 5.2 fusion.659
  525.8 9.2 collective-permute-done.7
  535.1 75.4 %conditional.19 = (f32[768,2304]{1,0:T(8,128)}, f32[768,768]{1,0:T(8,128)}, f32[768,3072]{1,0:T(8,128)}, f32[3072,768]{1,0:T(8,128)}, f32[9216]{0:T(1024)S(1)}, /*index=5*/f32[1,256,768]{2,1,0:T(8,128)}) conditional(s32[]{:T(128)} %convert_element_type.1071, () %tuple.172, (bf16[2,256,768]{2,1,0:T(8,128)(2,1)S(1)}, s32[]{:T(128)}, ...), branch_computations={%region_128.129_spmd, %region_129.150_spmd} | conditional | flops 10416083968 | bytes 246396208 | solution.py:264
  541.7 3.2 fusion.716
  550.1 4.1 fusion.750
  554.1 2.4 convolution_convert_fusion.14
  558.1 4.0 convolution_add_fusion.18
  562.2 9.9 convert_reduce_fusion.29
  572.1 2.2 multiply_reduce_fusion.30
  578.4 2.6 convolution_convert_fusion.12
  590.6 4.2 fusion.699
  594.8 10.2 %fusion.669 = f32[3072,768]{1,0:T(8,128)} fusion(f32[256,3072]{1,0:T(8,128)S(1)} %copy-done.232, f32[256,768]{1,0:T(8,128)S(1)} %copy-done.59), kind=kOutput, calls=%fused_computation.999 | convolution fusion | flops 1259274240 | bytes 13369344 | tf_op jit(solution)/shard_map/cond/branch_1_fun/dot_general | solution.py:23
  605.0 5.2 fusion.718
  611.3 2.9 copy.246
  614.3 7.0 add_bitcast_fusion.3
  621.4 15.6 %add_bitcast_fusion.2 = f32[1,768,2304]{2,1,0:T(8,128)} fusion(f32[768,2304]{1,0:T(8,128)} %get-tuple-element.1255, f32[768,2304]{1,0:T(8,128)} %get-tuple-element.1254, f32[768,2304]{1,0:T(8,128)} %get-tuple-element.1253, f32[768,2304]{1,0:T(8,128)} %get-tuple-element.1251, f32[768,2304]{1,0:T(8,128)} %get-tuple-element.1252), kind=kLoop, calls=%fused_computation.1094 | loop fusion | flops 7077888 | bytes 42467328 | tf_op jit(solution)/shard_map/broadcast_in_dim | solution.py:278
  637.1 21.0 %add_bitcast_fusion.1 = f32[1,768,3072]{2,1,0:T(8,128)} fusion(f32[768,3072]{1,0:T(8,128)} %get-tuple-element.1265, f32[768,3072]{1,0:T(8,128)} %get-tuple-element.1264, f32[768,3072]{1,0:T(8,128)} %get-tuple-element.1263, f32[768,3072]{1,0:T(8,128)} %get-tuple-element.1261, f32[768,3072]{1,0:T(8,128)} %get-tuple-element.1262), kind=kLoop, calls=%fused_computation.1093 | loop fusion | flops 9437184 | bytes 56623104 | tf_op jit(solution)/shard_map/broadcast_in_dim | solution.py:280
  658.2 20.0 %add_bitcast_fusion = f32[1,3072,768]{2,1,0:T(8,128)} fusion(f32[3072,768]{1,0:T(8,128)} %get-tuple-element.1270, f32[3072,768]{1,0:T(8,128)} %get-tuple-element.1269, f32[3072,768]{1,0:T(8,128)} %get-tuple-element.1268, f32[3072,768]{1,0:T(8,128)} %get-tuple-element.1266, f32[3072,768]{1,0:T(8,128)} %get-tuple-element.1267), kind=kLoop, calls=%fused_computation.1092 | loop fusion | flops 9437184 | bytes 56623104 | tf_op jit(solution)/shard_map/broadcast_in_dim | solution.py:281
  686.5 2.3 copy.247
  688.8 15.0 %reduce-scatter.10.cloned.1.call-done = f32[1,96,768]{2,1,0:T(8,128)} async-done(((f32[1,768,768]{2,1,0:T(8,128)}), f32[1,96,768]{2,1,0:T(8,128)}) %reduce-scatter.10.cloned.1.call-update) | async-done | bytes 294928 | tf_op jit(solution)/shard_map/reduce_scatter | solution.py:279
  703.8 79.3 %reduce-scatter.8.cloned.1.call-done = f32[1,96,2304]{2,1,0:T(8,128)} async-done(((f32[1,768,2304]{2,1,0:T(8,128)}), f32[1,96,2304]{2,1,0:T(8,128)}) %reduce-scatter.8.cloned.1.call-update) | async-done | bytes 884752 | tf_op jit(solution)/shard_map/reduce_scatter | solution.py:278
  783.1 100.7 %reduce-scatter.12.cloned.1.call-done = f32[1,96,3072]{2,1,0:T(8,128)} async-done(((f32[1,768,3072]{2,1,0:T(8,128)}), f32[1,96,3072]{2,1,0:T(8,128)}) %reduce-scatter.12.cloned.1.call-update) | async-done | bytes 1179664 | tf_op jit(solution)/shard_map/reduce_scatter | solution.py:280
  883.8 100.6 %reduce-scatter.14.cloned.1.call-done = f32[1,384,768]{2,1,0:T(8,128)} async-done(((f32[1,3072,768]{2,1,0:T(8,128)}), f32[1,384,768]{2,1,0:T(8,128)}) %reduce-scatter.14.cloned.1.call-update) | async-done | bytes 1179664 | tf_op jit(solution)/shard_map/reduce_scatter | solution.py:281
  (444 shorter events, 108.7 us)
Async XLA Ops:
  7.2 679.3 %reduce-scatter.16.cloned.1.call-start = ((), (), s32[]{:S(2)}) async-start(), calls=%async_computation.9 | async-start | bytes 5308416
  8.3 31.3 %copy-start.26 = (bf16[2,1,256,768]{3,2,1,0:T(8,128)(2,1)S(1)}, bf16[2,1,256,768]{3,2,1,0:T(8,128)(2,1)}, u32[]{:S(2)}) copy-start(bf16[2,1,256,768]{3,2,1,0:T(8,128)(2,1)} %param.28) | copy-start | bytes 2359300
  37.3 11.2 %copy-start = (bf16[1,768,768]{2,1,0:T(8,128)(2,1)S(1)}, bf16[1,768,768]{2,1,0:T(8,128)(2,1)}, u32[]{:S(2)}) copy-start(bf16[1,768,768]{2,1,0:T(8,128)(2,1)} %param.31) | copy-start | bytes 3538948
  37.3 11.2 %copy-start.30 = (f32[1,9216]{1,0:T(1,128)S(1)}, f32[1,9216]{1,0:T(1,128)}, u32[]{:S(2)}) copy-start(f32[1,9216]{1,0:T(1,128)} %param.34) | copy-start | bytes 110596
  37.4 11.2 %copy-start.222 = (s32[2,1]{0,1:T(1,128)S(1)}, s32[2,1]{0,1:T(1,128)}, u32[]{:S(2)}) copy-start(s32[2,1]{0,1:T(1,128)} %param.29) | copy-start | bytes 28
  37.4 11.0 %collective-permute-start = (bf16[256,768]{1,0:T(8,128)(2,1)}, bf16[256,768]{1,0:T(8,128)(2,1)}, u32[]{:S(2)}, u32[]{:S(2)}) collective-permute-start(bf16[256,768]{1,0:T(8,128)(2,1)} %get-tuple-element.1239), channel_id=1, source_target_pairs={{0,8},{8,16},{16,24},{1,9},{9,17},{17,25},{2,10},{10,18},{18,26},{... | collective-permute-start | bytes 1179656 | tf_op jit(solution)/shard_map/ppermute | solution.py:19
  84.2 14.1 %copy-start.80 = (bf16[1,256,768]{2,1,0:T(8,128)(2,1)}, bf16[1,256,768]{2,1,0:T(8,128)(2,1)S(1)}, u32[]{:S(2)}) copy-start(bf16[1,256,768]{2,1,0:T(8,128)(2,1)S(1)} %get-tuple-element.1240) | copy-start | bytes 1179652
  84.2 14.1 %collective-permute-start.1 = (bf16[256,768]{1,0:T(8,128)(2,1)}, bf16[256,768]{1,0:T(8,128)(2,1)}, u32[]{:S(2)}, u32[]{:S(2)}) collective-permute-start(bf16[256,768]{1,0:T(8,128)(2,1)} %get-tuple-element.1241), channel_id=1, source_target_pairs={{0,8},{8,16},{16,24},{1,9},{9,17},{17,25},{2,10},{10,18},{18,26},{... | collective-permute-start | bytes 1179656 | tf_op jit(solution)/shard_map/ppermute | solution.py:19
  99.7 47.9 %copy-start.82 = (bf16[1,256,768]{2,1,0:T(8,128)(2,1)}, bf16[1,256,768]{2,1,0:T(8,128)(2,1)S(1)}, u32[]{:S(2)}) copy-start(bf16[1,256,768]{2,1,0:T(8,128)(2,1)S(1)} %get-tuple-element.1242) | copy-start | bytes 1179652
  99.7 47.9 %collective-permute-start.2 = (bf16[256,768]{1,0:T(8,128)(2,1)}, bf16[256,768]{1,0:T(8,128)(2,1)}, u32[]{:S(2)}, u32[]{:S(2)}) collective-permute-start(bf16[256,768]{1,0:T(8,128)(2,1)} %get-tuple-element.1243), channel_id=1, source_target_pairs={{0,8},{8,16},{16,24},{1,9},{9,17},{17,25},{2,10},{10,18},{18,26},{... | collective-permute-start | bytes 1179656 | tf_op jit(solution)/shard_map/ppermute | solution.py:19
  148.8 13.3 %copy-start.83 = (bf16[1,256,768]{2,1,0:T(8,128)(2,1)}, bf16[1,256,768]{2,1,0:T(8,128)(2,1)S(1)}, u32[]{:S(2)}) copy-start(bf16[1,256,768]{2,1,0:T(8,128)(2,1)S(1)} %get-tuple-element.1244) | copy-start | bytes 1179652
  148.8 12.3 %collective-permute-start.3 = (bf16[256,768]{1,0:T(8,128)(2,1)}, bf16[256,768]{1,0:T(8,128)(2,1)}, u32[]{:S(2)}, u32[]{:S(2)}) collective-permute-start(bf16[256,768]{1,0:T(8,128)(2,1)} %get-tuple-element.1245), channel_id=1, source_target_pairs={{0,8},{8,16},{16,24},{1,9},{9,17},{17,25},{2,10},{10,18},{18,26},{... | collective-permute-start | bytes 1179656 | tf_op jit(solution)/shard_map/ppermute | solution.py:19
  183.1 48.1 %copy-start.9 = (pred[256,768]{1,0:T(32,128)(4,1)S(1)}, pred[256,768]{1,0:T(32,128)(4,1)}, u32[]{:S(2)}) copy-start(pred[256,768]{1,0:T(32,128)(4,1)} %copy-done.8) | copy-start | bytes 589828
  183.1 48.1 %copy-start.31 = (f32[1,9216]{1,0:T(1,128)S(1)}, f32[1,9216]{1,0:T(1,128)}, u32[]{:S(2)}) copy-start(f32[1,9216]{1,0:T(1,128)} %param.34) | copy-start | bytes 110596
  183.1 48.1 %copy-start.223 = (s32[2,1]{0,1:T(1,128)S(1)}, s32[2,1]{0,1:T(1,128)}, u32[]{:S(2)}) copy-start(s32[2,1]{0,1:T(1,128)} %param.29) | copy-start | bytes 28
  184.0 47.0 %collective-permute-start.4 = (bf16[256,768]{1,0:T(8,128)(2,1)S(1)}, bf16[256,768]{1,0:T(8,128)(2,1)S(1)}, u32[]{:S(2)}, u32[]{:S(2)}) collective-permute-start(bf16[256,768]{1,0:T(8,128)(2,1)S(1)} %convert_element_type.1063), channel_id=1, source_target_pairs={{8,0},{16,8},{24,16},{9,1},{17,9},{25,17},{10,2},{18,10},{26,18},{... | collective-permute-start | bytes 1179656 | tf_op jit(solution)/shard_map/ppermute | solution.py:19
  252.1 11.4 %collective-permute-start.5 = (bf16[256,768]{1,0:T(8,128)(2,1)S(1)}, bf16[256,768]{1,0:T(8,128)(2,1)S(1)}, u32[]{:S(2)}, u32[]{:S(2)}) collective-permute-start(bf16[256,768]{1,0:T(8,128)(2,1)S(1)} %convert_element_type.1066), channel_id=1, source_target_pairs={{8,0},{16,8},{24,16},{9,1},{17,9},{25,17},{10,2},{18,10},{26,18},{... | collective-permute-start | bytes 1179656 | tf_op jit(solution)/shard_map/ppermute | solution.py:19
  284.7 160.8 %collective-permute-start.6 = (bf16[256,768]{1,0:T(8,128)(2,1)S(1)}, bf16[256,768]{1,0:T(8,128)(2,1)S(1)}, u32[]{:S(2)}, u32[]{:S(2)}) collective-permute-start(bf16[256,768]{1,0:T(8,128)(2,1)S(1)} %convert_element_type.1069), channel_id=1, source_target_pairs={{8,0},{16,8},{24,16},{9,1},{17,9},{25,17},{10,2},{18,10},{26,18},{... | collective-permute-start | bytes 1179656 | tf_op jit(solution)/shard_map/ppermute | solution.py:19
  445.5 5.9 copy-start.34
  450.8 25.3 %copy-start.54 = (f32[256,768]{1,0:T(8,128)}, f32[256,768]{1,0:T(8,128)S(1)}, u32[]{:S(2)}) copy-start(f32[256,768]{1,0:T(8,128)S(1)} %get-tuple-element.1327) | copy-start | bytes 2359300 | tf_op jit(solution)/shard_map/cond
  452.6 4.0 copy-start.168
  471.6 16.8 %copy-start.6 = (f32[256,768]{1,0:T(8,128)}, f32[256,768]{1,0:T(8,128)S(1)}, u32[]{:S(2)}) copy-start(f32[256,768]{1,0:T(8,128)S(1)} %get-tuple-element.1488) | copy-start | bytes 2359300 | tf_op jit(solution)/shard_map/cond
  471.6 16.7 %copy-start.151 = (f32[256]{0:T(256)}, f32[256]{0:T(256)S(1)}, u32[]{:S(2)}) copy-start(f32[256]{0:T(256)S(1)} %broadcast_multiply_fusion.32) | copy-start | bytes 3076 | tf_op jit(solution)/shard_map/cond
  471.6 4.5 slice-start.16
  471.9 16.5 %copy-start.193 = (f32[256]{0:T(256)}, f32[256]{0:T(256)S(1)}, u32[]{:S(2)}) copy-start(f32[256]{0:T(256)S(1)} %add_rsqrt_fusion.16) | copy-start | bytes 3076 | tf_op jit(solution)/shard_map/cond
  471.9 4.3 slice-start.17
  471.9 14.2 %slice-start.6 = ((s8[4718592]{0:T(1024)(128)(4,1)}), s8[4194304]{0:T(1024)(128)(4,1)S(1)}, s32[]{:S(2)}) async-start(s8[4718592]{0:T(1024)(128)(4,1)} %bitcast.745), calls=%async_computation.16 | async-start | bytes 8388608 | tf_op jit(solution)/shard_map/cond
  476.2 10.0 %copy-start.229 = (f32[256,3072]{1,0:T(8,128)}, f32[256,3072]{1,0:T(8,128)S(1)}, u32[]{:S(2)}) copy-start(f32[256,3072]{1,0:T(8,128)S(1)} %convolution_add_fusion.16) | copy-start | bytes 9437188 | tf_op jit(solution)/shard_map/cond
  476.2 10.0 %slice-start.7 = ((s8[4718592]{0:T(1024)(128)(4,1)}), s8[524288]{0:T(1024)(128)(4,1)S(1)}, s32[]{:S(2)}) async-start(s8[4718592]{0:T(1024)(128)(4,1)} %bitcast.745), calls=%async_computation.17 | async-start | bytes 1048576 | tf_op jit(solution)/shard_map/cond
  492.5 4.7 copy-start.159
  503.4 4.5 copy-start.129
  503.7 4.2 copy-start.56
  503.8 4.2 copy-start.230
  507.9 9.9 %copy-start.7 = (f32[256,768]{1,0:T(8,128)S(1)}, f32[256,768]{1,0:T(8,128)}, u32[]{:S(2)}) copy-start(f32[256,768]{1,0:T(8,128)} %copy-done.6) | copy-start | bytes 2359300 | tf_op jit(solution)/shard_map/cond
  507.9 9.9 %copy-start.102 = (bf16[256,3072]{1,0:T(8,128)(2,1)S(1)}, bf16[256,3072]{1,0:T(8,128)(2,1)}, u32[]{:S(2)}) copy-start(bf16[256,3072]{1,0:T(8,128)(2,1)} %copy-done.101) | copy-start | bytes 4718596 | tf_op jit(solution)/shard_map/cond
  507.9 9.9 %copy-start.152 = (f32[256]{0:T(256)S(1)}, f32[256]{0:T(256)}, u32[]{:S(2)}) copy-start(f32[256]{0:T(256)} %copy-done.151) | copy-start | bytes 3076 | tf_op jit(solution)/shard_map/cond
  508.0 9.9 copy-start.194
  517.9 5.3 copy-start.130
  524.5 10.6 %collective-permute-start.7 = (bf16[256,768]{1,0:T(8,128)(2,1)S(1)}, bf16[256,768]{1,0:T(8,128)(2,1)S(1)}, u32[]{:S(2)}, u32[]{:S(2)}) collective-permute-start(bf16[256,768]{1,0:T(8,128)(2,1)S(1)} %convert_element_type.1072), channel_id=1, source_target_pairs={{8,0},{16,8},{24,16},{9,1},{17,9},{25,17},{10,2},{18,10},{26,18},{... | collective-permute-start | bytes 1179656 | tf_op jit(solution)/shard_map/ppermute | solution.py:19
  535.1 5.3 copy-start.35
  540.4 21.7 %copy-start.57 = (f32[256,768]{1,0:T(8,128)}, f32[256,768]{1,0:T(8,128)S(1)}, u32[]{:S(2)}) copy-start(f32[256,768]{1,0:T(8,128)S(1)} %get-tuple-element.1331) | copy-start | bytes 2359300 | tf_op jit(solution)/shard_map/cond
  540.4 4.5 copy-start.185
  546.7 7.4 copy-start.70
  548.0 6.1 copy-start.76
  557.8 16.5 %copy-start.153 = (f32[256]{0:T(256)}, f32[256]{0:T(256)S(1)}, u32[]{:S(2)}) copy-start(f32[256]{0:T(256)S(1)} %broadcast_multiply_fusion.38) | copy-start | bytes 3076 | tf_op jit(solution)/shard_map/cond
  557.9 4.3 slice-start.18
  558.1 16.2 %copy-start.195 = (f32[256]{0:T(256)}, f32[256]{0:T(256)S(1)}, u32[]{:S(2)}) copy-start(f32[256]{0:T(256)S(1)} %add_rsqrt_fusion.18) | copy-start | bytes 3076 | tf_op jit(solution)/shard_map/cond
  558.1 4.0 slice-start.19
  558.1 13.9 %slice-start.8 = ((s8[4718592]{0:T(1024)(128)(4,1)}), s8[4194304]{0:T(1024)(128)(4,1)S(1)}, s32[]{:S(2)}) async-start(s8[4718592]{0:T(1024)(128)(4,1)} %bitcast.747), calls=%async_computation.18 | async-start | bytes 8388608 | tf_op jit(solution)/shard_map/cond
  562.1 9.9 copy-start.231
  562.2 9.9 slice-start.9
  578.4 4.8 copy-start.160
  589.3 5.5 copy-start.133
  590.6 4.2 copy-start.59
  590.6 4.2 copy-start.232
  594.8 10.2 %copy-start.104 = (bf16[256,3072]{1,0:T(8,128)(2,1)S(1)}, bf16[256,3072]{1,0:T(8,128)(2,1)}, u32[]{:S(2)}) copy-start(bf16[256,3072]{1,0:T(8,128)(2,1)} %copy-done.103) | copy-start | bytes 4718596 | tf_op jit(solution)/shard_map/cond
  594.8 10.2 %copy-start.154 = (f32[256]{0:T(256)S(1)}, f32[256]{0:T(256)}, u32[]{:S(2)}) copy-start(f32[256]{0:T(256)} %copy-done.153) | copy-start | bytes 3076 | tf_op jit(solution)/shard_map/cond
  594.8 10.2 %copy-start.196 = (f32[256]{0:T(256)S(1)}, f32[256]{0:T(256)}, u32[]{:S(2)}) copy-start(f32[256]{0:T(256)} %copy-done.195) | copy-start | bytes 3076 | tf_op jit(solution)/shard_map/cond
  605.0 5.3 copy-start.134
  614.3 89.5 %reduce-scatter.10.cloned.1.call-start = ((), (), s32[]{:S(2)}) async-start(), calls=%async_computation.6 | async-start | bytes 2654208 | tf_op jit(solution)/shard_map/reduce_scatter | solution.py:279
  621.4 161.7 %reduce-scatter.8.cloned.1.call-start = ((), (), s32[]{:S(2)}) async-start(), calls=%async_computation.5 | async-start | bytes 7962624 | tf_op jit(solution)/shard_map/reduce_scatter | solution.py:278
  637.1 246.7 %reduce-scatter.12.cloned.1.call-start = ((), (), s32[]{:S(2)}) async-start(), calls=%async_computation.7 | async-start | bytes 10616832 | tf_op jit(solution)/shard_map/reduce_scatter | solution.py:280
  658.2 326.2 %reduce-scatter.14.cloned.1.call-start = ((), (), s32[]{:S(2)}) async-start(), calls=%async_computation.8 | async-start | bytes 10616832 | tf_op jit(solution)/shard_map/reduce_scatter | solution.py:281
  686.5 297.9 %copy-start.61 = (f32[1,2,1,256,768]{4,3,2,1,0:T(8,128)}, f32[1,2,1,256,768]{4,3,2,1,0:T(8,128)S(1)}, u32[]{:S(2)}) copy-start(f32[1,2,1,256,768]{4,3,2,1,0:T(8,128)S(1)} %bitcast_dynamic-update-slice_fusion) | copy-start | bytes 4718596
  (66 other events, 116.7 us)
Sparse Core Ops, SparseCore 0:
  614.4 51.8 reduce-scatter.15
  669.2 34.5 reduce-scatter.9
  706.7 76.3 reduce-scatter.7
  785.8 97.8 reduce-scatter.11
  886.5 97.8 reduce-scatter.13
where the time goes:
time: 1000 us; the launch traced here: 991 us
  waiting for transfers between devices  550 us (55%)
  matrix products  157 us (16%)
  local copies, waits for them, and re-layouts  95.4 us (10%)
  other arithmetic  90.4 us (9%)
  starting transfers between devices  60.6 us (6%)
  loops' own time  23.5 us (2%)
  between operations  15 us (2%)
    ppermute x8, waiting for transfers between devices, shifted(): return lax.ppermute(x, axis, pairs)  254 us
    dot_general x28, matrix products, matmul(): return jnp.dot(left, right, preferred_element_type=jnp.float32)  123 us
    reduce_scatter x1, waiting for transfers between devices, shards(): lax.psum_scatter(totals[2][None], 'dp', scatter_dimension=1, tiled=True)  101 us
    reduce_scatter x1, waiting for transfers between devices, shards(): lax.psum_scatter(totals[3][None], 'dp', scatter_dimension=1, tiled=True)  101 us
    reduce_scatter x1, waiting for transfers between devices, shards(): lax.psum_scatter(totals[0][None], 'dp', scatter_dimension=1, tiled=True)  79.3 us
    ppermute x8, starting transfers between devices, shifted(): return lax.ppermute(x, axis, pairs)  60.4 us
    broadcast_in_dim x1, other arithmetic, shards(): totals[2][None]  21 us
    another operation x5, loops' own time, shards(): lax.cond(active, lambda: backward_parts(block_in, key_valid, weights, vec...  20.3 us
  transfers between devices with their start and end apart: 13, of which 12 were waited for; matrix products, arithmetic and copies ran while one was open for 7% of the time, Pallas kernels for 0%

commit v1 on v0

v1 whole, which is shorter than its diff:
```python
from functools import partial

import jax
import jax.numpy as jnp
from jax import lax
from jax.experimental import pallas as pl
from jax.experimental.pallas import tpu as pltpu
from jax.sharding import PartitionSpec as P

HEAD_DIM = 64
EPS = 1e-06
F32 = jnp.float32
BF16 = jnp.bfloat16
MESH = pl.DeviceIdType.MESH


def nn(left, right):
    return jnp.dot(left, right, preferred_element_type=F32)


def nt(left, right):
    return lax.dot_general(left, right, (((1,), (1,)), ((), ())), preferred_element_type=F32)


def tn(left, right):
    return lax.dot_general(left, right, (((0,), (0,)), ((), ())), preferred_element_type=F32)


def normalize(hidden):
    centered = hidden - jnp.mean(hidden, axis=-1, keepdims=True)
    inverse = lax.rsqrt(jnp.mean(centered * centered, axis=-1, keepdims=True) + EPS)
    return centered * inverse, inverse


def norm_back(grad, unit, inverse):
    average = jnp.mean(grad, axis=-1, keepdims=True)
    slope = jnp.mean(grad * unit, axis=-1, keepdims=True)
    return inverse * (grad - average - unit * slope)


def gelu_pair(u):
    phi = 0.5 + 0.5 * lax.erf(u * 0.7071067811865476)
    density = jnp.exp(u * u * -0.5) * 0.3989422804014327
    return u * phi, phi + u * density


class Refs:
    def __init__(self, names, refs):
        self.__dict__.update(zip(names, refs))


INPUTS = ("patches", "lengths", "wqkv_h", "wout_h", "wup_h", "wdown_h", "vec", "cot")
OUTPUTS = ("outputs", "input_grads", "gqkv", "gout", "gup", "gdown", "gvec")


def scratch_plan(micro, rows, width, hidden):
    heads = width // HEAD_DIM
    dma = pltpu.SemaphoreType.DMA
    vm = pltpu.VMEM
    act = vm((micro, rows, width), BF16)
    return dict(
        wqkv=vm((width, 3 * width), BF16),
        wout=vm((width, width), BF16),
        wup=vm((width, hidden), BF16),
        wdown=vm((hidden, width), BF16),
        x=act, a1=act, n1=act, o=act, n2=act, a2=act, y=act, e=act, eo=act, f=act,
        r1=vm((micro, rows, 128), F32),
        r2=vm((micro, rows, 128), F32),
        qkv=vm((micro, rows, 3 * width), BF16),
        bias=vm((1, 3 * width), F32),
        p=vm((micro, heads, rows, rows), BF16),
        rl=vm((micro, rows, width), F32),
        of=vm((micro, rows, width), F32),
        g=vm((micro, rows, hidden), BF16),
        gp=vm((micro, rows, hidden), BF16),
        du=vm((micro, rows, hidden), BF16),
        dp=vm((micro, rows, 3 * width), BF16),
        do=vm((rows, width), BF16),
        doo=vm((rows, width), BF16),
        rest=vm((rows, width), BF16),
        h1=vm((rows, width), F32),
        da=vm((rows, width), F32),
        ig=vm((micro, rows, width), F32),
        stage=vm((2, width, width), BF16),
        wsem=dma((4,)),
        psem=dma((micro,)),
        csem=dma((micro,)),
        xsend=dma((micro,)),
        xrecv=dma((micro,)),
        esend=dma((micro,)),
        erecv=dma((micro,)),
        osem=dma((micro,)),
        isem=dma((micro,)),
        gsem=dma((2,)),
    )


def pair_masks():
    lane = lax.broadcasted_iota(jnp.int32, (1, 128), 1)
    return (lane < HEAD_DIM).astype(BF16), (lane >= HEAD_DIM).astype(BF16), lane < HEAD_DIM


def forward_attention(k, m, key_bias, width):
    rows = k.x.shape[1]
    vec = k.vec
    unit, inverse = normalize(k.x[m].astype(F32))
    k.n1[m] = unit.astype(BF16)
    k.r1[m] = jnp.broadcast_to(inverse, (rows, 128))
    k.a1[m] = (unit * (1.0 + vec[:, :width]) + vec[:, width : 2 * width]).astype(BF16)
    normed = k.a1[m]
    for c in range(0, 3 * width, 256):
        k.qkv[m, :, c : c + 256] = (nn(normed, k.wqkv[:, c : c + 256]) + k.bias[:, c : c + 256]).astype(BF16)
    low, high, first = pair_masks()
    ones = jnp.ones((rows, 128), BF16)
    for c in range(0, width, 128):
        queries = k.qkv[m, :, c : c + 128]
        keys = k.qkv[m, :, width + c : width + c + 128]
        values = jnp.concatenate([k.qkv[m, :, 2 * width + c : 2 * width + c + 128], ones], axis=1)
        sums = []
        for half, mask in enumerate((low, high)):
            scores = nt(queries * (mask * jnp.asarray(HEAD_DIM**-0.5, BF16)), keys) + key_bias
            top = jnp.max(scores, axis=-1, keepdims=True)
            raised = jnp.exp(scores - top).astype(BF16)
            k.p[m, c // HEAD_DIM + half] = raised
            sums.append(nn(raised, values))
        inverse_sum = 1.0 / jnp.where(first, sums[0][:, 128:], sums[1][:, 128:])
        k.rl[m, :, c : c + 128] = inverse_sum
        joined = jnp.where(first, sums[0][:, :128], sums[1][:, :128]) * inverse_sum
        k.of[m, :, c : c + 128] = joined
        k.o[m, :, c : c + 128] = joined.astype(BF16)
    attended = k.o[m]
    for c in range(0, width, 256):
        k.h1[:, c : c + 256] = k.x[m, :, c : c + 256].astype(F32) + (
            nn(attended, k.wout[:, c : c + 256]) + vec[:, 4 * width + c : 4 * width + c + 256]
        )
    unit, inverse = normalize(k.h1[...])
    k.n2[m] = unit.astype(BF16)
    k.r2[m] = jnp.broadcast_to(inverse, (rows, 128))
    k.a2[m] = (unit * (1.0 + vec[:, 5 * width : 6 * width]) + vec[:, 6 * width : 7 * width]).astype(BF16)


def forward_mlp(k, m, width, hidden):
    vec = k.vec
    normed = k.a2[m]
    for c in range(0, hidden, 256):
        u = nn(normed, k.wup[:, c : c + 256]) + vec[:, 8 * width + c : 8 * width + c + 256]
        value, slope = gelu_pair(u)
        k.g[m, :, c : c + 256] = value.astype(BF16)
        k.gp[m, :, c : c + 256] = slope.astype(BF16)
    activated = k.g[m]
    k.y[m] = (k.h1[...] + (nn(activated, k.wdown[...]) + vec[:, 7 * width : 8 * width])).astype(BF16)


def add_vector(k, at, value):
    k.gvec[:, at : at + value.shape[1]] += value


def backward_chain(k, m, width, hidden):
    rows = k.x.shape[1]
    vec = k.vec
    grad = k.e[m]
    for c in range(0, hidden, 256):
        k.du[m, :, c : c + 256] = (
            nt(grad, k.wdown[c : c + 256, :]) * k.gp[m, :, c : c + 256].astype(F32)
        ).astype(BF16)
    grad_two = nt(k.du[m], k.wup[...])
    unit = k.n2[m].astype(F32)
    add_vector(k, 5 * width, jnp.sum(grad_two * unit, axis=0, keepdims=True))
    add_vector(k, 6 * width, jnp.sum(grad_two, axis=0, keepdims=True))
    grad_mid = k.e[m].astype(F32) + norm_back(
        grad_two * (1.0 + vec[:, 5 * width : 6 * width]), unit, k.r2[m, :, :1]
    )
    k.h1[...] = grad_mid
    k.f[m] = grad_mid.astype(BF16)
    branch = k.f[m]
    k.do[...] = (nt(branch, k.wout[...]) * k.rl[m]).astype(BF16)
    product = k.do[...].astype(F32) * k.of[m]
    k.doo[...] = product.astype(BF16)
    k.rest[...] = (product - k.doo[...].astype(F32)).astype(BF16)
    low, high, first = pair_masks()
    minus = jnp.full((rows, 128), -1.0, BF16)
    scale = HEAD_DIM**-0.5
    for c in range(0, width, 128):
        queries = k.qkv[m, :, c : c + 128]
        keys = k.qkv[m, :, width + c : width + c + 128]
        values = jnp.concatenate([k.qkv[m, :, 2 * width + c : 2 * width + c + 128], minus], axis=1)
        grads = k.do[:, c : c + 128]
        inner = k.doo[:, c : c + 128]
        rest = pltpu.roll(k.rest[:, c : c + 128].astype(F32), HEAD_DIM, 1).astype(BF16)
        inners = (jnp.where(first, inner, rest), jnp.where(first, rest, inner))
        total_q = total_k = total_v = 0.0
        for half, mask in enumerate((low, high)):
            raised = k.p[m, c // HEAD_DIM + half]
            left = jnp.concatenate([grads * mask, inners[half]], axis=1)
            grad_scores = (raised.astype(F32) * nt(left, values)).astype(BF16)
            total_v = total_v + tn(raised, grads * mask)
            total_q = total_q + nn(grad_scores, keys * mask)
            total_k = total_k + tn(grad_scores, queries * mask)
        k.dp[m, :, c : c + 128] = (total_q * scale).astype(BF16)
        k.dp[m, :, width + c : width + c + 128] = (total_k * scale).astype(BF16)
        k.dp[m, :, 2 * width + c : 2 * width + c + 128] = total_v.astype(BF16)
    grad_one = nt(k.dp[m], k.wqkv[...])
    unit = k.n1[m].astype(F32)
    add_vector(k, 0, jnp.sum(grad_one * unit, axis=0, keepdims=True))
    add_vector(k, width, jnp.sum(grad_one, axis=0, keepdims=True))
    grad_in = k.h1[...] + norm_back(grad_one * (1.0 + vec[:, :width]), unit, k.r1[m, :, :1])
    k.ig[m] = grad_in
    k.eo[m] = grad_in.astype(BF16)


def pipeline_kernel(scratch_names, *refs):
    k = Refs(INPUTS + OUTPUTS + scratch_names, refs)
    sec = lax.axis_index("section")
    count = lax.axis_size("section")
    micro, rows, width = k.x.shape
    hidden = k.wup.shape[1]
    is_first = sec == 0
    is_last = sec == count - 1
    after = jnp.minimum(sec + 1, count - 1)
    before = jnp.maximum(sec - 1, 0)

    barrier = pltpu.get_barrier_semaphore()

    @pl.when(sec > 0)
    def _():
        pl.semaphore_signal(barrier, inc=1, device_id={"section": before}, device_id_type=MESH)

    @pl.when(sec < count - 1)
    def _():
        pl.semaphore_signal(barrier, inc=1, device_id={"section": after}, device_id_type=MESH)

    def patch_copy(m):
        return pltpu.make_async_copy(k.patches.at[m], k.x.at[m], k.psem.at[m])

    def cot_copy(m):
        return pltpu.make_async_copy(k.cot.at[m], k.e.at[m], k.csem.at[m])

    loads = [
        pltpu.make_async_copy(src.at[0], dst, k.wsem.at[i])
        for i, (src, dst) in enumerate(
            ((k.wqkv_h, k.wqkv), (k.wout_h, k.wout), (k.wup_h, k.wup), (k.wdown_h, k.wdown))
        )
    ]

    @pl.when(is_first)
    def _():
        for m in range(micro):
            patch_copy(m).start()

    for load in loads:
        load.start()

    @pl.when(is_last)
    def _():
        for m in range(micro):
            cot_copy(m).start()

    k.bias[:, : width] = k.vec[:, 2 * width : 3 * width]
    k.bias[:, width : 2 * width] = jnp.zeros((1, width), F32)
    k.bias[:, 2 * width :] = k.vec[:, 3 * width : 4 * width]
    k.gvec[...] = jnp.zeros_like(k.gvec)
    loads[0].wait()
    loads[1].wait()

    def y_send(m):
        return pltpu.make_async_remote_copy(
            src_ref=k.y.at[m], dst_ref=k.x.at[m], send_sem=k.xsend.at[m], recv_sem=k.xrecv.at[m],
            device_id={"section": after}, device_id_type=MESH,
        )

    def e_send(m):
        return pltpu.make_async_remote_copy(
            src_ref=k.eo.at[m], dst_ref=k.e.at[m], send_sem=k.esend.at[m], recv_sem=k.erecv.at[m],
            device_id={"section": before}, device_id_type=MESH,
        )

    def out_copy(m):
        return pltpu.make_async_copy(k.y.at[m], k.outputs.at[m], k.osem.at[m])

    def in_copy(m):
        return pltpu.make_async_copy(k.ig.at[m], k.input_grads.at[m], k.isem.at[m])

    pl.semaphore_wait(
        barrier, (sec > 0).astype(jnp.int32) + (sec < count - 1).astype(jnp.int32)
    )

    def forward_step(m, carry):
        @pl.when(is_first)
        def _():
            patch_copy(m).wait()

        @pl.when(sec > 0)
        def _():
            y_send(m).wait_recv()

        key_bias = jnp.where(
            lax.broadcasted_iota(jnp.int32, (1, rows), 1) < k.lengths[m, 0], 0.0, -1e30
        )
        forward_attention(k, m, key_bias, width)

        @pl.when(m == 0)
        def _():
            loads[2].wait()
            loads[3].wait()

        forward_mlp(k, m, width, hidden)

        @pl.when(sec < count - 1)
        def _():
            y_send(m).start()

        out_copy(m).start()
        return carry

    lax.fori_loop(0, micro, forward_step, 0)

    def backward_step(m, carry):
        @pl.when(is_last)
        def _():
            cot_copy(m).wait()
            valid = lax.broadcasted_iota(jnp.int32, (rows, width), 0) < k.lengths[m, 0]
            k.e[m] = jnp.where(valid, k.e[m].astype(F32), 0.0).astype(BF16)

        @pl.when(sec < count - 1)
        def _():
            e_send(m).wait_recv()

        backward_chain(k, m, width, hidden)

        @pl.when(sec > 0)
        def _():
            e_send(m).start()

        in_copy(m).start()
        return carry

    lax.fori_loop(0, micro, backward_step, 0)

    both = micro * rows
    ones = jnp.ones((16, both), BF16)

    def joined(ref, *at):
        return ref[at if at else ...].reshape(both, -1)

    def column_sums(value):
        return nn(ones, value)[:1]

    pending = [None, None]
    turn = 0

    def emit(value, target):
        nonlocal turn
        slot = turn % 2
        if pending[slot] is not None:
            pending[slot].wait()
        k.stage[slot] = value.astype(BF16)
        copy = pltpu.make_async_copy(k.stage.at[slot], target, k.gsem.at[slot])
        copy.start()
        pending[slot] = copy
        turn += 1

    add_vector(k, 7 * width, column_sums(joined(k.e)))
    add_vector(k, 4 * width, column_sums(joined(k.f)))
    for c in range(0, hidden, width):
        grads = k.du[:, :, c : c + width].reshape(both, width)
        emit(tn(joined(k.a2), grads), k.gup.at[:, pl.ds(c, width)])
        add_vector(k, 8 * width + c, column_sums(grads))
    for c in range(0, hidden, width):
        emit(tn(k.g[:, :, c : c + width].reshape(both, width), joined(k.e)), k.gdown.at[pl.ds(c, width)])
    for part in range(3):
        c = part * width
        grads = k.dp[:, :, c : c + width].reshape(both, width)
        emit(tn(joined(k.a1), grads), k.gqkv.at[:, pl.ds(c, width)])
        if part != 1:
            add_vector(k, (2 if part == 0 else 3) * width, column_sums(grads))
    emit(tn(joined(k.o), joined(k.f)), k.gout)
    for copy in pending:
        copy.wait()
    for m in range(micro):
        out_copy(m).wait()
        in_copy(m).wait()

        @pl.when(sec < count - 1)
        def _():
            y_send(m).wait_send()

        @pl.when(sec > 0)
        def _():
            e_send(m).wait_send()


def shards(patches, lengths, qkv_weight, out_weight, up_weight, down_weight, vectors, cotangent):
    micro, _, rows, width = patches.shape
    hidden = up_weight.shape[2]
    plan = scratch_plan(micro, rows, width, hidden)
    anywhere = pl.BlockSpec(memory_space=pl.ANY)
    in_vmem = pl.BlockSpec(memory_space=pltpu.VMEM)
    results = pl.pallas_call(
        partial(pipeline_kernel, tuple(plan)),
        out_shape=(
            jax.ShapeDtypeStruct((micro, rows, width), BF16),
            jax.ShapeDtypeStruct((micro, rows, width), F32),
            jax.ShapeDtypeStruct((width, 3 * width), BF16),
            jax.ShapeDtypeStruct((width, width), BF16),
            jax.ShapeDtypeStruct((width, hidden), BF16),
            jax.ShapeDtypeStruct((hidden, width), BF16),
            jax.ShapeDtypeStruct(vectors.shape, F32),
        ),
        in_specs=[
            anywhere,
            pl.BlockSpec(memory_space=pltpu.SMEM),
            anywhere,
            anywhere,
            anywhere,
            anywhere,
            in_vmem,
            anywhere,
        ],
        out_specs=(anywhere,) * 6 + (in_vmem,),
        scratch_shapes=list(plan.values()),
        compiler_params=pltpu.CompilerParams(
            collective_id=0, has_side_effects=True, vmem_limit_bytes=60 << 20
        ),
    )(
        patches[:, 0],
        lengths,
        qkv_weight,
        out_weight,
        up_weight,
        down_weight,
        vectors,
        cotangent[:, 0],
    )
    outputs, input_grads, *grads, vector_grad = results
    collected = [
        lax.psum_scatter(grad[None], "dp", scatter_dimension=1, tiled=True).astype(F32)
        for grad in grads
    ]
    return (
        outputs[None, :, None],
        input_grads[None, :, None],
        *collected,
        lax.psum_scatter(vector_grad, "dp", scatter_dimension=1, tiled=True),
    )


def solution(mesh):
    placed = (
        P(None, "dp", None, None),
        P(None, "dp"),
        P("section", None, None),
        P("section", None, None),
        P("section", None, None),
        P("section", None, None),
        P("section", None),
        P(None, "dp", None, None),
    )
    return jax.shard_map(
        shards,
        mesh=mesh,
        in_specs=placed,
        out_specs=(
            P("section", None, "dp", None, None),
            P("section", None, "dp", None, None),
            P("section", "dp", None),
            P("section", "dp", None),
            P("section", "dp", None),
            P("section", "dp", None),
            P("section", "dp"),
        ),
        check_vma=False,
    )
```

time: 1000 us -> 416 us (0.42)
  waiting for transfers between devices: 550 us -> 236 us
  matrix products: 157 us -> 0 us
  Pallas kernels: 0 us -> 149 us
  local copies, waits for them, and re-layouts: 95.4 us -> 8.89 us
  other arithmetic: 90.4 us -> 7.95 us
  starting transfers between devices: 60.6 us -> 0.19 us
  loops' own time: 23.5 us -> 0 us
    ppermute x8 -> x0, waiting for transfers between devices: 254 us -> none  [shifted(): return lax.ppermute(x, axis, pairs)]
    pallas_call x0 -> x1, Pallas kernels: none -> 149 us  [shards(): pl.pallas_call(partial(pipeline_kernel, tuple(plan)), out_shape=(jax.Shap...]
    dot_general x40 -> x0, matrix products: 141 us -> none  [the longest x28 123 us: matmul(): return jnp.dot(left, right, preferred_element_type=jnp.float32)]
    reduce_scatter x4, waiting for transfers between devices: 296 us -> 181 us  [shards(): lax.psum_scatter(grad[None], 'dp', scatter_dimension=1, tiled=True)]
    broadcast_in_dim x5 -> x0, other arithmetic: 65 us -> none  [the longest x1 21 us: shards(): totals[2][None]]
    ppermute x8 -> x0, starting transfers between devices: 60.4 us -> none  [shifted(): return lax.ppermute(x, axis, pairs)]
    unnamed x6, waiting for transfers between devices: 0.1 us -> 54.5 us
    broadcast_in_dim x19 -> x0, local copies, waits for them, and re-layouts: 41.8 us -> none  [the longest x3 14.2 us: shards(): jnp.zeros(weights[2].shape, jnp.float32)]
  transfers between devices with their start and end apart: 13 -> 5, of which waited for: 12 -> 5; matrix products, arithmetic and copies ran while one was open for 7% -> 2% of each run, Pallas kernels for 0% -> 0%
where the time goes in v1:
time: 416 us
  waiting for transfers between devices  236 us (57%)
  Pallas kernels  149 us (36%)
  between operations  13.8 us (3%)
  local copies, waits for them, and re-layouts  8.89 us (2%)
  other arithmetic  7.95 us (2%)
    reduce_scatter x4, waiting for transfers between devices, shards(): lax.psum_scatter(grad[None], 'dp', scatter_dimension=1, tiled=True)  181 us
    pallas_call x1, Pallas kernels, shards(): pl.pallas_call(partial(pipeline_kernel, tuple(plan)), out_shape=(jax.Shap...  149 us
    unnamed x6, waiting for transfers between devices  54.5 us
    unnamed x9, local copies, waits for them, and re-layouts  8.89 us
  transfers between devices with their start and end apart: 5, of which 5 were waited for; matrix products, arithmetic and copies ran while one was open for 2% of the time, Pallas kernels for 0%

profile of v1, /device:TPU:0, one launch (start us, length us, event | category | flops | bytes accessed | tf_op | source)
XLA Modules:
  0.0 415.6 jit_solution(13887550159545540582)
XLA Ops:
  7.2 0.0 reduce-scatter.16.cloned.1.call-start
  7.2 1.3 copy.18.refs_1_
  8.5 148.8 %shard_map.135 = (bf16[2,256,768]{2,1,0:T(8,128)(2,1)}, f32[2,256,768]{2,1,0:T(8,128)}, bf16[768,2304]{1,0:T(8,128)(2,1)}, bf16[768,768]{1,0:T(8,128)(2,1)}, bf1...) custom-call(bf16[2,256,768]{2,1,0:T(8,128)(2,1)} %bitcast.20, s32[2,1]{1,0:T(2,128)} %copy.18.refs_1_, ...), custom_call_target="tpu_custom_call" | custom-call | tf_op jit(solution)/shard_map/pallas_call | solution.py:398
  157.3 3.7 copy.21
  161.0 0.0 reduce-scatter.16.cloned.1.call-update
  161.0 0.0 reduce-scatter.10.cloned.1.call-start
  161.1 0.7 reduce-scatter.10.cloned.1.call-update
  161.8 0.0 reduce-scatter.8.cloned.1.call-start
  161.8 0.7 reduce-scatter.8.cloned.1.call-update
  162.5 0.0 reduce-scatter.14.cloned.1.call-start
  162.6 0.5 reduce-scatter.14.cloned.1.call-update
  163.1 0.0 reduce-scatter.12.cloned.1.call-start
  163.1 0.5 reduce-scatter.12.cloned.1.call-update
  163.7 0.0 copy-start.1
  163.7 52.1 %reduce-scatter.16.cloned.1.call-done = f32[1152,1]{1,0:T(8,128)} async-done(((f32[9216,1]{1,0:T(8,128)}), f32[1152,1]{1,0:T(8,128)}) %reduce-scatter.16.cloned.1.call-update) | async-done | bytes 4624
  215.8 1.9 copy.22
  217.6 0.0 copy-start
  217.6 31.4 %reduce-scatter.10.cloned.1.call-done = bf16[1,96,768]{2,1,0:T(8,128)(2,1)} async-done(((bf16[1,768,768]{2,1,0:T(8,128)(2,1)}), bf16[1,96,768]{2,1,0:T(8,128)(2,1)}) %reduce-scatter.10.cloned.1.call-update) | async-done | bytes 147472 | tf_op jit(solution)/shard_map/reduce_scatter | solution.py:436
  249.1 1.6 convert_element_type.13
  250.7 42.8 %reduce-scatter.8.cloned.1.call-done = bf16[1,96,2304]{2,1,0:T(8,128)(2,1)} async-done(((bf16[1,768,2304]{2,1,0:T(8,128)(2,1)}), bf16[1,96,2304]{2,1,0:T(8,128)(2,1)}) %reduce-scatter.8.cloned.1.call-update) | async-done | bytes 442384 | tf_op jit(solution)/shard_map/reduce_scatter | solution.py:436
  293.5 2.0 convert_element_type.12
  295.5 53.8 %reduce-scatter.14.cloned.1.call-done = bf16[1,384,768]{2,1,0:T(8,128)(2,1)} async-done(((bf16[1,3072,768]{2,1,0:T(8,128)(2,1)}), bf16[1,384,768]{2,1,0:T(8,128)(2,1)}) %reduce-scatter.14.cloned.1.call-update) | async-done | bytes 589840 | tf_op jit(solution)/shard_map/reduce_scatter | solution.py:436
  349.3 2.2 convert_element_type.15
  351.4 53.4 %reduce-scatter.12.cloned.1.call-done = bf16[1,96,3072]{2,1,0:T(8,128)(2,1)} async-done(((bf16[1,768,3072]{2,1,0:T(8,128)(2,1)}), bf16[1,96,3072]{2,1,0:T(8,128)(2,1)}) %reduce-scatter.12.cloned.1.call-update) | async-done | bytes 589840 | tf_op jit(solution)/shard_map/reduce_scatter | solution.py:436
  404.9 2.2 convert_element_type.14
  407.1 0.0 copy-done.1
  407.1 0.9 copy.25
  408.0 0.0 copy-done
  408.0 1.1 copy.26
Async XLA Ops:
  7.2 208.6 %reduce-scatter.16.cloned.1.call-start = ((), (), s32[]{:S(2)}) async-start(), calls=%async_computation.9 | async-start | bytes 5308416
  161.0 88.0 %reduce-scatter.10.cloned.1.call-start = ((), (), s32[]{:S(2)}) async-start(), calls=%async_computation.6 | async-start | bytes 1327104 | tf_op jit(solution)/shard_map/reduce_scatter | solution.py:436
  161.8 131.8 %reduce-scatter.8.cloned.1.call-start = ((), (), s32[]{:S(2)}) async-start(), calls=%async_computation.5 | async-start | bytes 3981312 | tf_op jit(solution)/shard_map/reduce_scatter | solution.py:436
  162.5 186.8 %reduce-scatter.14.cloned.1.call-start = ((), (), s32[]{:S(2)}) async-start(), calls=%async_computation.8 | async-start | bytes 5308416 | tf_op jit(solution)/shard_map/reduce_scatter | solution.py:436
  163.1 241.8 %reduce-scatter.12.cloned.1.call-start = ((), (), s32[]{:S(2)}) async-start(), calls=%async_computation.7 | async-start | bytes 5308416 | tf_op jit(solution)/shard_map/reduce_scatter | solution.py:436
  163.7 243.4 %copy-start.1 = (bf16[2,256,768]{2,1,0:T(8,128)(2,1)S(1)}, bf16[2,256,768]{2,1,0:T(8,128)(2,1)}, u32[]{:S(2)}) copy-start(bf16[2,256,768]{2,1,0:T(8,128)(2,1)} %get-tuple-element.14) | copy-start | bytes 2359300
  217.6 190.3 %copy-start = (f32[2,256,768]{2,1,0:T(8,128)S(1)}, f32[2,256,768]{2,1,0:T(8,128)}, u32[]{:S(2)}) copy-start(f32[2,256,768]{2,1,0:T(8,128)} %get-tuple-element.15) | copy-start | bytes 4718596
Sparse Core Ops, SparseCore 0:
  161.2 54.5 reduce-scatter.15
  218.0 30.9 reduce-scatter.9
  251.4 42.1 reduce-scatter.7
  295.8 53.4 reduce-scatter.13
  351.6 53.3 reduce-scatter.11

commit v2 on v1

v2 whole, which is shorter than its diff:
```python
from functools import partial

import jax
import jax.numpy as jnp
from jax import lax
from jax.experimental import pallas as pl
from jax.experimental.pallas import tpu as pltpu
from jax.sharding import PartitionSpec as P

HEAD_DIM = 64
EPS = 1e-06
F32 = jnp.float32
BF16 = jnp.bfloat16
MESH = pl.DeviceIdType.MESH


def nn(left, right):
    return jnp.dot(left, right, preferred_element_type=F32)


def nt(left, right):
    return lax.dot_general(left, right, (((1,), (1,)), ((), ())), preferred_element_type=F32)


def tn(left, right):
    return lax.dot_general(left, right, (((0,), (0,)), ((), ())), preferred_element_type=F32)


def normalize(hidden):
    centered = hidden - jnp.mean(hidden, axis=-1, keepdims=True)
    inverse = lax.rsqrt(jnp.mean(centered * centered, axis=-1, keepdims=True) + EPS)
    return centered * inverse, inverse


def norm_back(grad, unit, inverse):
    average = jnp.mean(grad, axis=-1, keepdims=True)
    slope = jnp.mean(grad * unit, axis=-1, keepdims=True)
    return inverse * (grad - average - unit * slope)


def gelu_pair(u):
    phi = 0.5 + 0.5 * lax.erf(u * 0.7071067811865476)
    density = jnp.exp(u * u * -0.5) * 0.3989422804014327
    return u * phi, phi + u * density


class Refs:
    def __init__(self, names, refs):
        self.__dict__.update(zip(names, refs))


INPUTS = ("patches", "lengths", "wqkv_h", "wout_h", "wup_h", "wdown_h", "vec", "cot")
RESULTS = ("outputs", "input_grads", "qkv_grad", "out_grad", "up_grad", "down_grad", "vector_grad")


def scratch_plan(micro, rows, width, hidden, chips, peers, fused):
    heads = width // HEAD_DIM
    dma = pltpu.SemaphoreType.DMA
    vm = pltpu.VMEM
    act = vm((micro, rows, width), BF16)
    blocks = vm((micro, chips, rows, width), BF16)
    plan = dict(
        wqkv=vm((width, 3 * width), BF16),
        wout=vm((width, width), BF16),
        wup=vm((width, hidden), BF16),
        wdown=vm((hidden, width), BF16),
        x=act, a1=act, n1=act, o=act, n2=act, y=act, a2=blocks, e=blocks,
        r1=vm((micro, rows, 128), F32),
        r2=vm((micro, rows, 128), F32),
        qkv=vm((micro, rows, 3 * width), BF16),
        bias=vm((1, 3 * width), F32),
        p=vm((micro, heads, rows, rows), BF16),
        wide=vm((rows, hidden), BF16),
        gp=vm((micro, rows, hidden), BF16),
        dp=vm((micro, rows, 3 * width), BF16),
        do=vm((rows, width), BF16),
        doo=vm((rows, width), BF16),
        rest=vm((rows, width), BF16),
        pool=vm((2 * width, width), F32),
        ig=vm((micro, rows, width), F32),
        wsem=dma((4,)),
        psem=dma((micro,)),
        csem=dma((micro,)),
        xsend=dma((micro,)),
        xrecv=dma((micro,)),
        esend=dma((micro,)),
        erecv=dma((micro,)),
        osem=dma((micro,)),
        isem=dma((micro,)),
        gsem=dma((3 * chips,)),
    )
    if fused:
        share = width // peers
        plan.update(
            gvec=vm((1, 8 * width + hidden), F32),
            asend=dma((2, micro, chips)),
            arecv=dma((micro, chips)),
            bsend=dma((2, micro, chips)),
            brecv=dma((micro, chips)),
            prx=vm((4, chips, share, width), BF16),
            pxsend=dma((4, chips)),
            pxrecv=dma((4, chips)),
            rsx=vm((2, 4, chips - 1, share, width), BF16),
            rsend=dma((2, 4, chips)),
            rrecv=dma((2, 4, chips)),
            vrx=vm((peers, 1, (8 * width + hidden) // peers), F32),
            vsend=dma((peers,)),
            vrecv=dma((peers,)),
            upx=vm((chips, 2, share, width), BF16),
            uprx=vm((chips, share, width), BF16),
            upsem=dma((2,)),
            dnx=vm((hidden // peers, width), BF16),
            dnrx=vm((hidden // peers, width), BF16),
            dnsem=dma((2,)),
            uax=vm((chips, share, width), BF16),
            uasend=dma((chips,)),
            uarecv=dma((chips,)),
        )
    return plan


def pair_masks():
    lane = lax.broadcasted_iota(jnp.int32, (1, 128), 1)
    return (lane < HEAD_DIM).astype(BF16), (lane >= HEAD_DIM).astype(BF16), lane < HEAD_DIM


def pool_rows(k, block, m=0):
    rows = k.x.shape[1]
    return pl.ds(pl.multiple_of((block + m) * rows, rows), rows)


RL, OF, MID = 0, 2, 4


def forward_attention(k, m, z, key_bias):
    rows, width = k.x.shape[1:]
    vec = k.vec
    unit, inverse = normalize(k.x[m].astype(F32))
    k.n1[m] = unit.astype(BF16)
    k.r1[m] = jnp.broadcast_to(inverse, (rows, 128))
    k.a1[m] = (unit * (1.0 + vec[:, :width]) + vec[:, width : 2 * width]).astype(BF16)
    normed = k.a1[m]
    for c in range(0, 3 * width, 256):
        k.qkv[m, :, c : c + 256] = (nn(normed, k.wqkv[:, c : c + 256]) + k.bias[:, c : c + 256]).astype(BF16)
    low, high, first = pair_masks()
    ones = jnp.ones((rows, 128), BF16)
    for c in range(0, width, 128):
        queries = k.qkv[m, :, c : c + 128]
        keys = k.qkv[m, :, width + c : width + c + 128]
        values = jnp.concatenate([k.qkv[m, :, 2 * width + c : 2 * width + c + 128], ones], axis=1)
        sums = []
        for half, mask in enumerate((low, high)):
            scores = nt(queries * (mask * jnp.asarray(HEAD_DIM**-0.5, BF16)), keys) + key_bias
            top = jnp.max(scores, axis=-1, keepdims=True)
            raised = jnp.exp(scores - top).astype(BF16)
            k.p[m, c // HEAD_DIM + half] = raised
            sums.append(nn(raised, values))
        inverse_sum = 1.0 / jnp.where(first, sums[0][:, 128:], sums[1][:, 128:])
        k.pool[pool_rows(k, RL, m), c : c + 128] = inverse_sum
        joined = jnp.where(first, sums[0][:, :128], sums[1][:, :128]) * inverse_sum
        k.pool[pool_rows(k, OF, m), c : c + 128] = joined
        k.o[m, :, c : c + 128] = joined.astype(BF16)
    attended = k.o[m]
    mid = pool_rows(k, MID)
    for c in range(0, width, 256):
        k.pool[mid, c : c + 256] = k.x[m, :, c : c + 256].astype(F32) + (
            nn(attended, k.wout[:, c : c + 256]) + vec[:, 4 * width + c : 4 * width + c + 256]
        )
    unit, inverse = normalize(k.pool[mid, :])
    k.n2[m] = unit.astype(BF16)
    k.r2[m] = jnp.broadcast_to(inverse, (rows, 128))
    k.a2[m, z] = (unit * (1.0 + vec[:, 5 * width : 6 * width]) + vec[:, 6 * width : 7 * width]).astype(BF16)


def forward_mlp(k, m, z):
    width = k.x.shape[2]
    vec = k.vec
    normed = k.a2[m, z]
    for c in range(0, k.wup.shape[1], 256):
        u = nn(normed, k.wup[:, c : c + 256]) + vec[:, 8 * width + c : 8 * width + c + 256]
        value, slope = gelu_pair(u)
        k.wide[:, c : c + 256] = value.astype(BF16)
        k.gp[m, :, c : c + 256] = slope.astype(BF16)
    added = nn(k.wide[...], k.wdown[...]) + vec[:, 7 * width : 8 * width]
    k.y[m] = (k.pool[pool_rows(k, MID), :] + added).astype(BF16)


def add_sums(ref, at, value):
    ref[:, at : at + value.shape[1]] += jnp.sum(value, axis=0, keepdims=True)


def backward_mlp(k, gvec, m, z):
    width = k.x.shape[2]
    vec = k.vec
    grad = k.e[m, z]
    add_sums(gvec, 7 * width, grad.astype(F32))
    for c in range(0, k.wup.shape[1], 256):
        grad_up = (
            nt(grad, k.wdown[c : c + 256, :]) * k.gp[m, :, c : c + 256].astype(F32)
        ).astype(BF16)
        k.wide[:, c : c + 256] = grad_up
        add_sums(gvec, 8 * width + c, grad_up.astype(F32))
    grad_two = nt(k.wide[...], k.wup[...])
    unit = k.n2[m].astype(F32)
    add_sums(gvec, 5 * width, grad_two * unit)
    add_sums(gvec, 6 * width, grad_two)
    grad_mid = k.e[m, z].astype(F32) + norm_back(
        grad_two * (1.0 + vec[:, 5 * width : 6 * width]), unit, k.r2[m, :, :1]
    )
    k.pool[pool_rows(k, MID), :] = grad_mid
    branch = grad_mid.astype(BF16)
    k.x[m] = branch
    add_sums(gvec, 4 * width, branch.astype(F32))


def backward_attention(k, gvec, m):
    rows, width = k.x.shape[1:]
    vec = k.vec
    k.do[...] = (nt(k.x[m], k.wout[...]) * k.pool[pool_rows(k, RL, m), :]).astype(BF16)
    product = k.do[...].astype(F32) * k.pool[pool_rows(k, OF, m), :]
    k.doo[...] = product.astype(BF16)
    k.rest[...] = (product - k.doo[...].astype(F32)).astype(BF16)
    low, high, first = pair_masks()
    minus = jnp.full((rows, 128), -1.0, BF16)
    scale = HEAD_DIM**-0.5
    for c in range(0, width, 128):
        queries = k.qkv[m, :, c : c + 128]
        keys = k.qkv[m, :, width + c : width + c + 128]
        values = jnp.concatenate([k.qkv[m, :, 2 * width + c : 2 * width + c + 128], minus], axis=1)
        grads = k.do[:, c : c + 128]
        inner = k.doo[:, c : c + 128]
        rest = pltpu.roll(k.rest[:, c : c + 128].astype(F32), HEAD_DIM, 1).astype(BF16)
        inners = (jnp.where(first, inner, rest), jnp.where(first, rest, inner))
        total_q = total_k = total_v = 0.0
        for half, mask in enumerate((low, high)):
            raised = k.p[m, c // HEAD_DIM + half]
            left = jnp.concatenate([grads * mask, inners[half]], axis=1)
            grad_scores = (raised.astype(F32) * nt(left, values)).astype(BF16)
            total_v = total_v + tn(raised, grads * mask)
            total_q = total_q + nn(grad_scores, keys * mask)
            total_k = total_k + tn(grad_scores, queries * mask)
        grad_q = (total_q * scale).astype(BF16)
        grad_v = total_v.astype(BF16)
        k.dp[m, :, c : c + 128] = grad_q
        k.dp[m, :, width + c : width + c + 128] = (total_k * scale).astype(BF16)
        k.dp[m, :, 2 * width + c : 2 * width + c + 128] = grad_v
        add_sums(gvec, 2 * width + c, grad_q.astype(F32))
        add_sums(gvec, 3 * width + c, grad_v.astype(F32))
    grad_one = nt(k.dp[m], k.wqkv[...])
    unit = k.n1[m].astype(F32)
    add_sums(gvec, 0, grad_one * unit)
    add_sums(gvec, width, grad_one)
    grad_in = k.pool[pool_rows(k, MID), :] + norm_back(
        grad_one * (1.0 + vec[:, :width]), unit, k.r1[m, :, :1]
    )
    k.ig[m] = grad_in
    k.y[m] = grad_in.astype(BF16)


def attention_weight_grads(k, after_chunk):
    micro, rows, width = k.x.shape
    both = micro * rows
    normed = k.a1[...].reshape(both, width)
    for part in range(3):
        grads = k.dp[:, :, part * width : (part + 1) * width].reshape(both, width)
        k.wqkv[:, part * width : (part + 1) * width] = tn(normed, grads).astype(BF16)
        after_chunk(part)
    k.wout[...] = tn(k.o[...].reshape(both, width), k.x[...].reshape(both, width)).astype(BF16)
    after_chunk(3)


def mlp_weight_grads(k, origin, start, fresh):
    micro, rows, width = k.x.shape
    both = micro * rows
    normed = k.a2[:, origin].reshape(both, width)
    grad = k.e[:, origin].reshape(both, width)
    for c in range(0, width, 256):
        at = pl.ds(pl.multiple_of(start + c, 256), 256)
        u = nn(normed, k.wup[:, at]) + k.vec[:, pl.ds(pl.multiple_of(8 * width + start + c, 256), 256)]
        value, slope = gelu_pair(u)
        grad_up = (nt(grad, k.wdown[at, :]) * slope).astype(BF16)
        up = tn(normed, grad_up)
        down = tn(value.astype(BF16), grad)
        if fresh:
            k.pool[:width, c : c + 256] = up
            k.pool[width + c : width + c + 256, :] = down
        else:
            k.pool[:width, c : c + 256] += up
            k.pool[width + c : width + c + 256, :] += down


def pipeline_kernel(scratch_names, fused, *refs):
    k = Refs(INPUTS + RESULTS + scratch_names, refs)
    sec = lax.axis_index("section")
    count = lax.axis_size("section")
    peers = lax.axis_size("dp")
    me = lax.axis_index("dp")
    micro, rows, width = k.x.shape
    hidden = k.wup.shape[1]
    chips = k.e.shape[1]
    z, core = (me // 2, me % 2) if fused else (0, 0)
    gvec = k.gvec if fused else k.vector_grad
    share = width // peers
    is_first = sec == 0
    is_last = sec == count - 1
    not_last = sec < count - 1
    after = jnp.minimum(sec + 1, count - 1)
    before = jnp.maximum(sec - 1, 0)

    barrier = pltpu.get_barrier_semaphore()

    @pl.when(sec > 0)
    def _():
        pl.semaphore_signal(barrier, inc=1, device_id={"section": before}, device_id_type=MESH)

    @pl.when(not_last)
    def _():
        pl.semaphore_signal(barrier, inc=1, device_id={"section": after}, device_id_type=MESH)

    if fused:
        for step in range(1, peers):
            pl.semaphore_signal(
                barrier, inc=1, device_id={"dp": (me + step) % peers}, device_id_type=MESH
            )

    def patch_copy(m):
        return pltpu.make_async_copy(k.patches.at[m], k.x.at[m], k.psem.at[m])

    def cot_copy(m):
        return pltpu.make_async_copy(k.cot.at[m], k.e.at[m, z], k.csem.at[m])

    loads = [
        pltpu.make_async_copy(src.at[0], dst, k.wsem.at[i])
        for i, (src, dst) in enumerate(
            ((k.wqkv_h, k.wqkv), (k.wout_h, k.wout), (k.wup_h, k.wup), (k.wdown_h, k.wdown))
        )
    ]

    @pl.when(is_first)
    def _():
        for m in range(micro):
            patch_copy(m).start()

    for load in loads:
        load.start()

    @pl.when(is_last)
    def _():
        for m in range(micro):
            cot_copy(m).start()

    k.bias[:, :width] = k.vec[:, 2 * width : 3 * width]
    k.bias[:, width : 2 * width] = jnp.zeros((1, width), F32)
    k.bias[:, 2 * width :] = k.vec[:, 3 * width : 4 * width]
    gvec[...] = jnp.zeros_like(gvec)
    loads[0].wait()
    loads[1].wait()

    def y_send(m):
        return pltpu.make_async_remote_copy(
            src_ref=k.y.at[m], dst_ref=k.x.at[m], send_sem=k.xsend.at[m], recv_sem=k.xrecv.at[m],
            device_id={"section": after}, device_id_type=MESH,
        )

    def e_send(m):
        return pltpu.make_async_remote_copy(
            src_ref=k.y.at[m], dst_ref=k.e.at[m, z], send_sem=k.esend.at[m], recv_sem=k.erecv.at[m],
            device_id={"section": before}, device_id_type=MESH,
        )

    def out_copy(m):
        return pltpu.make_async_copy(k.y.at[m], k.outputs.at[m], k.osem.at[m])

    def in_copy(m):
        return pltpu.make_async_copy(k.ig.at[m], k.input_grads.at[m], k.isem.at[m])

    def to_peer(src, dst, send, recv, device):
        return pltpu.make_async_remote_copy(
            src_ref=src, dst_ref=dst, send_sem=send, recv_sem=recv,
            device_id={"dp": device}, device_id_type=MESH,
        )

    def pass_on(ref, sends, recvs, m, origin, up):
        return to_peer(
            ref.at[m, origin], ref.at[m, origin], sends.at[0 if up else 1, m, origin],
            recvs.at[m, origin], me + 2 if up else me - 2,
        )

    def share_own(ref, sends, recvs, m):
        @pl.when(z < chips - 1)
        def _():
            pass_on(ref, sends, recvs, m, z, True).start()

        @pl.when(z > 0)
        def _():
            pass_on(ref, sends, recvs, m, z, False).start()

    def relay(ref, sends, recvs, m, distance):
        @pl.when(z >= distance)
        def _():
            pass_on(ref, sends, recvs, m, z - distance, True).wait_recv()

            @pl.when(z < chips - 1)
            def _():
                pass_on(ref, sends, recvs, m, z - distance, True).start()

        @pl.when(z + distance < chips)
        def _():
            pass_on(ref, sends, recvs, m, z + distance, False).wait_recv()

            @pl.when(z > 0)
            def _():
                pass_on(ref, sends, recvs, m, z + distance, False).start()

    def settle(ref, sends, recvs, m):
        for distance in range(chips):
            @pl.when((z >= distance) & (z < chips - 1))
            def _():
                pass_on(ref, sends, recvs, m, z - distance, True).wait_send()

            @pl.when((z + distance < chips) & (z > 0))
            def _():
                pass_on(ref, sends, recvs, m, z + distance, False).wait_send()

    if fused:
        acts = (k.a2, k.asend, k.arecv)
        errs = (k.e, k.bsend, k.brecv)
    arrivals = (sec > 0).astype(jnp.int32) + not_last.astype(jnp.int32)
    pl.semaphore_wait(barrier, arrivals + (peers - 1 if fused else 0))

    @pl.when(is_last)
    def _():
        for m in range(micro):
            cot_copy(m).wait()
            valid = lax.broadcasted_iota(jnp.int32, (rows, width), 0) < k.lengths[m, 0]
            k.e[m, z] = jnp.where(valid, k.e[m, z].astype(F32), 0.0).astype(BF16)
            if fused:
                share_own(*errs, m)
        if fused:
            for distance in range(1, chips - 1):
                for m in range(micro):
                    relay(*errs, m, distance)

    def forward_step(m, carry):
        @pl.when(is_first)
        def _():
            patch_copy(m).wait()

        @pl.when(sec > 0)
        def _():
            y_send(m).wait_recv()

        key_bias = jnp.where(
            lax.broadcasted_iota(jnp.int32, (1, rows), 1) < k.lengths[m, 0], 0.0, -1e30
        )
        forward_attention(k, m, z, key_bias)
        if fused:
            share_own(*acts, m)

        @pl.when(m == 0)
        def _():
            loads[2].wait()
            loads[3].wait()

        forward_mlp(k, m, z)

        @pl.when(not_last)
        def _():
            y_send(m).start()

        out_copy(m).start()
        return carry

    lax.fori_loop(0, micro, forward_step, 0)

    def relay_acts():
        for distance in range(1, chips - 1):
            for m in range(micro):
                relay(*acts, m, distance)

    if fused:
        pl.when(not_last)(relay_acts)

    for m in range(micro):
        out_copy(m).wait()

        @pl.when(not_last)
        def _():
            y_send(m).wait_send()

    def backward_step(m, carry):
        @pl.when(not_last)
        def _():
            e_send(m).wait_recv()
            if fused:
                share_own(*errs, m)

        backward_mlp(k, gvec, m, z)
        if fused:
            @pl.when(not_last & (m == micro - 1))
            def _():
                for early in range(micro - 1):
                    relay(*errs, early, 1)

        backward_attention(k, gvec, m)

        @pl.when(sec > 0)
        def _():
            e_send(m).start()

        in_copy(m).start()
        return carry

    lax.fori_loop(0, micro, backward_step, 0)

    def finish_hops():
        for m in range(micro):
            in_copy(m).wait()

            @pl.when(sec > 0)
            def _():
                e_send(m).wait_send()

    if not fused:
        attention_weight_grads(k, lambda part: None)
        for c in range(0, hidden, width):
            mlp_weight_grads(k, 0, c, True)
            k.wup[:, c : c + width] = k.pool[:width, :].astype(BF16)
            k.wdown[c : c + width, :] = k.pool[width:, :].astype(BF16)
        copies = [
            pltpu.make_async_copy(src, dst, k.wsem.at[i])
            for i, (src, dst) in enumerate(
                ((k.wqkv, k.qkv_grad), (k.wout, k.out_grad), (k.wup, k.up_grad), (k.wdown, k.down_grad))
            )
        ]
        for copy in copies:
            copy.start()
        for copy in copies:
            copy.wait()
        finish_hops()
        return

    sibling = me + 1 - 2 * core

    def part_rows(chip, parity):
        return pl.ds(pl.multiple_of(share * (2 * chip + parity), share), share)

    def part_ref(part, chip, parity):
        if part < 3:
            return k.wqkv.at[part_rows(chip, parity), pl.ds(part * width, width)]
        return k.wout.at[part_rows(chip, parity), :]

    def pair_copy(part, chip):
        return to_peer(
            part_ref(part, chip, 1 - core), k.prx.at[part, chip],
            k.pxsend.at[part, chip], k.pxrecv.at[part, chip], sibling,
        )

    def send_pair(part):
        for chip in range(chips):
            pair_copy(part, chip).start()

    attention_weight_grads(k, send_pair)

    length = gvec.shape[1] // peers

    def vector_copy(step):
        device = (me + step) % peers
        return to_peer(
            gvec.at[:, pl.ds(pl.multiple_of(device * length, 128), length)], k.vrx.at[step],
            k.vsend.at[step], k.vrecv.at[step], device,
        )

    for step in range(1, peers):
        vector_copy(step).start()

    def chain_copy(up, part, place):
        chip = place if up else chips - 1 - place
        lane = 0 if up else 1
        return to_peer(
            part_ref(part, chip, core), k.rsx.at[lane, part, place - 1],
            k.rsend.at[lane, part, place], k.rrecv.at[lane, part, place],
            me + 2 if up else me - 2,
        )

    def chain(stage, part):
        for up in (True, False):
            @pl.when((z if up else chips - 1 - z) == stage)
            def _():
                for place in range(chips - 1, stage, -1):
                    if stage > 0:
                        chain_copy(up, part, place).wait_recv()
                        chip = place if up else chips - 1 - place
                        target = part_ref(part, chip, core)
                        target[...] = (
                            target[...].astype(F32)
                            + k.rsx[0 if up else 1, part, place - 1].astype(F32)
                        ).astype(BF16)
                    chain_copy(up, part, place).start()

    for part in range(4):
        for chip in range(chips):
            pair_copy(part, chip).wait()
            target = part_ref(part, chip, core)
            target[...] = (target[...].astype(F32) + k.prx[part, chip].astype(F32)).astype(BF16)
        chain(0, part)

    @pl.when(not_last)
    def _():
        relay(*errs, micro - 1, 1)
        for m in range(micro):
            relay(*errs, m, 2)

    pl.when(is_last)(relay_acts)
    for m in range(micro):
        relay(*acts, m, chips - 1)

    def nearby(index):
        low = z + (index % 2) * (1 - 2 * (z % 2))
        return low + (index // 2) * (2 - 4 * ((low // 2) % 2))

    start = width * z
    mlp_weight_grads(k, z, start, True)
    chain(1, 0)
    chain(2, 0)
    mlp_weight_grads(k, nearby(1), start, False)
    chain(1, 1)
    chain(2, 1)
    for m in range(micro):
        relay(*errs, m, chips - 1)
    mlp_weight_grads(k, nearby(2), start, False)
    mlp_weight_grads(k, nearby(3), start, False)

    per_core = hidden // peers
    k.dnx[...] = k.pool[pl.ds(pl.multiple_of(width + per_core * (1 - core), per_core), per_core), :].astype(BF16)
    down_pair = to_peer(k.dnx, k.dnrx, k.dnsem.at[0], k.dnsem.at[1], sibling)
    down_pair.start()
    for chip in range(chips):
        for parity in range(2):
            k.upx[chip, parity] = k.pool[
                share * (2 * chip + parity) : share * (2 * chip + parity + 1), :
            ].astype(BF16)
    up_pair = to_peer(k.upx.at[:, 1 - core], k.uprx, k.upsem.at[0], k.upsem.at[1], sibling)
    up_pair.start()
    up_pair.wait()

    def spread(chip):
        return to_peer(
            k.upx.at[chip, core], k.uax.at[z], k.uasend.at[chip], k.uarecv.at[z], 2 * chip + core
        )

    def gathered(chip):
        return to_peer(
            k.upx.at[chip, core], k.uax.at[chip], k.uasend.at[chip], k.uarecv.at[chip], 2 * chip + core
        )

    finals = []
    for chip in range(chips):
        at = part_rows(chip, core)
        total = k.pool[at, :] + k.uprx[chip].astype(F32)
        k.pool[at, :] = total
        k.upx[chip, core] = total.astype(BF16)

        @pl.when(z != chip)
        def _():
            spread(chip).start()

    down_pair.wait()
    down_at = pl.ds(pl.multiple_of(width + per_core * core, per_core), per_core)
    k.pool[down_at, :] += k.dnrx[...].astype(F32)
    final = pltpu.make_async_copy(k.pool.at[down_at], k.down_grad, k.gsem.at[0])
    final.start()
    finals.append(final)

    for part in range(2, 4):
        chain(1, part)
        chain(2, part)
    for part in range(4):
        at = part_rows(part, 1 - core)
        k.pool[at, :] = part_ref(part, z, core)[...].astype(F32)

        @pl.when(z > 0)
        def _():
            chain_copy(True, part, z).wait_recv()
            k.pool[at, :] += k.rsx[0, part, z - 1].astype(F32)

        @pl.when(z < chips - 1)
        def _():
            chain_copy(False, part, chips - 1 - z).wait_recv()
            k.pool[at, :] += k.rsx[1, part, chips - 2 - z].astype(F32)

        target = k.qkv_grad.at[:, pl.ds(part * width, width)] if part < 3 else k.out_grad
        final = pltpu.make_async_copy(k.pool.at[at], target, k.gsem.at[1 + part])
        final.start()
        finals.append(final)
    for chip in range(chips):
        at = part_rows(chip, core)

        @pl.when(z != chip)
        def _():
            gathered(chip).wait_recv()
            k.pool[at, :] = k.uax[chip].astype(F32)

        final = pltpu.make_async_copy(
            k.pool.at[at], k.up_grad.at[:, pl.ds(chip * width, width)], k.gsem.at[5 + chip]
        )
        final.start()
        finals.append(final)
    own = gvec[:, pl.ds(pl.multiple_of(me * length, 128), length)]
    for step in range(1, peers):
        vector_copy(step).wait()
        own = own + k.vrx[step]
    k.vector_grad[...] = own

    for m in range(micro):
        settle(*acts, m)
        settle(*errs, m)
    for part in range(4):
        for up in (True, False):
            for place in range(1, chips):
                @pl.when((z if up else chips - 1 - z) < place)
                def _():
                    chain_copy(up, part, place).wait_send()
    for chip in range(chips):
        @pl.when(z != chip)
        def _():
            spread(chip).wait_send()
    for final in finals:
        final.wait()
    finish_hops()


def shards(patches, lengths, qkv_weight, out_weight, up_weight, down_weight, vectors, cotangent):
    micro, _, rows, width = patches.shape
    hidden = up_weight.shape[2]
    peers = lax.axis_size("dp")
    fused = peers == 8 and hidden == peers // 2 * width
    chips = peers // 2 if fused else 1
    plan = scratch_plan(micro, rows, width, hidden, chips, peers, fused)
    anywhere = pl.BlockSpec(memory_space=pl.ANY)
    in_vmem = pl.BlockSpec(memory_space=pltpu.VMEM)
    kept = F32 if fused else BF16
    cut = peers if fused else 1
    results = pl.pallas_call(
        partial(pipeline_kernel, tuple(plan), fused),
        out_shape=(
            jax.ShapeDtypeStruct((micro, rows, width), BF16),
            jax.ShapeDtypeStruct((micro, rows, width), F32),
            jax.ShapeDtypeStruct((width // cut, 3 * width), kept),
            jax.ShapeDtypeStruct((width // cut, width), kept),
            jax.ShapeDtypeStruct((width // cut, hidden), kept),
            jax.ShapeDtypeStruct((hidden // cut, width), kept),
            jax.ShapeDtypeStruct((1, vectors.shape[1] // cut), F32),
        ),
        in_specs=[
            anywhere,
            pl.BlockSpec(memory_space=pltpu.SMEM),
            anywhere,
            anywhere,
            anywhere,
            anywhere,
            in_vmem,
            anywhere,
        ],
        out_specs=(anywhere,) * 6 + (in_vmem,),
        scratch_shapes=list(plan.values()),
        compiler_params=pltpu.CompilerParams(
            collective_id=0, has_side_effects=True, vmem_limit_bytes=62 << 20
        ),
    )(
        patches[:, 0],
        lengths,
        qkv_weight,
        out_weight,
        up_weight,
        down_weight,
        vectors,
        cotangent[:, 0],
    )
    outputs, input_grads, *grads, vector_grad = results
    if fused:
        grads = [grad[None] for grad in grads]
    else:
        grads = [
            lax.psum_scatter(grad[None], "dp", scatter_dimension=1, tiled=True).astype(F32)
            for grad in grads
        ]
        vector_grad = lax.psum_scatter(vector_grad, "dp", scatter_dimension=1, tiled=True)
    return (outputs[None, :, None], input_grads[None, :, None], *grads, vector_grad)


def solution(mesh):
    placed = (
        P(None, "dp", None, None),
        P(None, "dp"),
        P("section", None, None),
        P("section", None, None),
        P("section", None, None),
        P("section", None, None),
        P("section", None),
        P(None, "dp", None, None),
    )
    return jax.shard_map(
        shards,
        mesh=mesh,
        in_specs=placed,
        out_specs=(
            P("section", None, "dp", None, None),
            P("section", None, "dp", None, None),
            P("section", "dp", None),
            P("section", "dp", None),
            P("section", "dp", None),
            P("section", "dp", None),
            P("section", "dp"),
        ),
        check_vma=False,
    )
```

time: 416 us -> 224 us (0.54)
  waiting for transfers between devices: 236 us -> 0 us
  Pallas kernels: 149 us -> 213 us
  between operations: 13.8 us -> 0.66 us
  other arithmetic: 7.95 us -> 0 us
    reduce_scatter x4 -> x0, waiting for transfers between devices: 181 us -> none  [shards(): lax.psum_scatter(grad[None], 'dp', scatter_dimension=1, tiled=True)]
    pallas_call x1, Pallas kernels: 149 us -> 213 us  [shards(): pl.pallas_call(partial(pipeline_kernel, tuple(plan), fused), out_shape=(j...]
    unnamed x6 -> x0, waiting for transfers between devices: 54.5 us -> none
    convert_element_type x4 -> x0, other arithmetic: 7.95 us -> none  [shards(): lax.psum_scatter(grad[None], 'dp', scatter_dimension=1, tiled=True)]
    unnamed x9 -> x20, local copies, waits for them, and re-layouts: 8.89 us -> 9.68 us
  transfers between devices with their start and end apart: 5 -> 0, of which waited for: 5 -> 0; matrix products, arithmetic and copies ran while one was open for 2% -> 0% of each run, Pallas kernels for 0% -> 0%
where the time goes in v2:
time: 224 us
  Pallas kernels  213 us (95%)
  local copies, waits for them, and re-layouts  9.68 us (4%)
    pallas_call x1, Pallas kernels, shards(): pl.pallas_call(partial(pipeline_kernel, tuple(plan), fused), out_shape=(j...  213 us
    unnamed x20, local copies, waits for them, and re-layouts  9.68 us

profile of v2, /device:TPU:0, one launch (start us, length us, event | category | flops | bytes accessed | tf_op | source)
XLA Modules:
  0.0 223.7 jit_solution(7553638328018225840)
XLA Ops:
  0.6 1.3 copy.15.refs_1_
  1.9 213.3 %shard_map.135 = (bf16[2,256,768]{2,1,0:T(8,128)(2,1)}, f32[2,256,768]{2,1,0:T(8,128)}, f32[96,2304]{1,0:T(8,128)}, f32[96,768]{1,0:T(8,128)}, f32[96,3072]{1,0:...) custom-call(bf16[2,256,768]{2,1,0:T(8,128)(2,1)} %bitcast.16, s32[2,1]{1,0:T(2,128)} %copy.15.refs_1_, ...), custom_call_target="tpu_custom_call" | custom-call | tf_op jit(solution)/shard_map/pallas_call | solution.py:744
  215.3 0.0 copy-start
  215.3 2.2 copy.25
  217.4 0.0 copy-done
  217.4 0.0 copy-start.3
  217.4 1.1 copy.26
  218.6 0.6 copy-done.3
  219.2 0.0 copy-start.4
  219.2 0.0 copy-start.2
  219.2 0.9 copy.27
  220.1 0.2 copy-done.4
  220.3 0.0 copy-start.1
  220.3 0.7 copy.28
  221.0 0.0 copy-done.2
  221.0 1.0 copy.29
  222.0 0.0 copy-done.1
  222.0 0.0 copy-start.5
  222.0 1.0 copy.30
  223.1 0.0 copy-done.5
  223.1 0.6 copy.31
Async XLA Ops:
  215.3 2.2 copy-start
  217.4 1.7 copy-start.3
  219.2 1.1 copy-start.4
  219.2 1.8 copy-start.2
  220.3 1.7 copy-start.1
  222.0 1.0 copy-start.5

commit v3 on v2

--- a/solution.py
+++ b/solution.py
@@ -78,6 +78,8 @@
         rest=vm((rows, width), BF16),
         pool=vm((2 * width, width), F32),
         ig=vm((micro, rows, width), F32),
+        lens=pltpu.SMEM((micro,), jnp.int32),
+        lsem=dma((1,)),
         wsem=dma((4,)),
         psem=dma((micro,)),
         csem=dma((micro,)),
@@ -115,6 +117,7 @@
             uax=vm((chips, share, width), BF16),
             uasend=dma((chips,)),
             uarecv=dma((chips,)),
+            turn=pltpu.SemaphoreType.REGULAR,
         )
     return plan
 
@@ -341,8 +344,10 @@
         for m in range(micro):
             patch_copy(m).start()
 
-    for load in loads:
-        load.start()
+    lens_copy = pltpu.make_async_copy(k.lengths, k.lens, k.lsem.at[0])
+    lens_copy.start()
+    loads[0].start()
+    loads[1].start()
 
     @pl.when(is_last)
     def _():
@@ -353,8 +358,11 @@
     k.bias[:, width : 2 * width] = jnp.zeros((1, width), F32)
     k.bias[:, 2 * width :] = k.vec[:, 3 * width : 4 * width]
     gvec[...] = jnp.zeros_like(gvec)
+    lens_copy.wait()
     loads[0].wait()
     loads[1].wait()
+    loads[2].start()
+    loads[3].start()
 
     def y_send(m):
         return pltpu.make_async_remote_copy(
@@ -432,7 +440,7 @@
     def _():
         for m in range(micro):
             cot_copy(m).wait()
-            valid = lax.broadcasted_iota(jnp.int32, (rows, width), 0) < k.lengths[m, 0]
+            valid = lax.broadcasted_iota(jnp.int32, (rows, width), 0) < k.lens[m]
             k.e[m, z] = jnp.where(valid, k.e[m, z].astype(F32), 0.0).astype(BF16)
             if fused:
                 share_own(*errs, m)
@@ -441,7 +449,9 @@
                 for m in range(micro):
                     relay(*errs, m, distance)
 
-    def forward_step(m, carry):
+    waits_turn = is_first & (core == 1) & not_last
+
+    def forward_step(m):
         @pl.when(is_first)
         def _():
             patch_copy(m).wait()
@@ -451,12 +461,16 @@
             y_send(m).wait_recv()
 
         key_bias = jnp.where(
-            lax.broadcasted_iota(jnp.int32, (1, rows), 1) < k.lengths[m, 0], 0.0, -1e30
+            lax.broadcasted_iota(jnp.int32, (1, rows), 1) < k.lens[m], 0.0, -1e30
         )
         forward_attention(k, m, z, key_bias)
         if fused:
             share_own(*acts, m)
 
+            @pl.when(waits_turn & (m > 0))
+            def _():
+                y_send(m - 1).start()
+
         @pl.when(m == 0)
         def _():
             loads[2].wait()
@@ -464,31 +478,20 @@
 
         forward_mlp(k, m, z)
 
-        @pl.when(not_last)
+        @pl.when(not_last & jnp.logical_not(waits_turn))
         def _():
             y_send(m).start()
 
         out_copy(m).start()
-        return carry
-
-    lax.fori_loop(0, micro, forward_step, 0)
-
-    def relay_acts():
-        for distance in range(1, chips - 1):
+
+    def relay_acts(*distances):
+        for distance in distances:
             for m in range(micro):
                 relay(*acts, m, distance)
 
-    if fused:
-        pl.when(not_last)(relay_acts)
-
-    for m in range(micro):
+    def backward_step(m):
         out_copy(m).wait()
 
-        @pl.when(not_last)
-        def _():
-            y_send(m).wait_send()
-
-    def backward_step(m, carry):
         @pl.when(not_last)
         def _():
             e_send(m).wait_recv()
@@ -497,10 +500,10 @@
 
         backward_mlp(k, gvec, m, z)
         if fused:
-            @pl.when(not_last & (m == micro - 1))
+            @pl.when(is_first & not_last & (m == micro - 1))
             def _():
                 for early in range(micro - 1):
-                    relay(*errs, early, 1)
+                    relay(*errs, early, 2)
 
         backward_attention(k, gvec, m)
 
@@ -509,9 +512,42 @@
             e_send(m).start()
 
         in_copy(m).start()
+        if fused:
+            @pl.when(is_first & not_last & (m < micro - 1))
+            def _():
+                relay(*errs, m, 1)
+
+    def turn_round():
+        if fused:
+            @pl.when(is_first & (core == 0) & not_last)
+            def _():
+                y_send(micro - 1).wait_send()
+                pl.semaphore_signal(k.turn, inc=1, device_id={"dp": me + 1}, device_id_type=MESH)
+
+            @pl.when(waits_turn)
+            def _():
+                pl.semaphore_wait(k.turn, 1)
+                y_send(micro - 1).start()
+        for m in range(micro):
+            waited = is_first & (core == 0) if fused and m == micro - 1 else False
+
+            @pl.when(jnp.logical_not(waited))
+            def _():
+                y_send(m).wait_send()
+
+        if fused:
+            relay_acts(1)
+            pl.when(sec < count - 2)(lambda: relay_acts(*range(2, chips - 1)))
+
+    def step(index, carry):
+        forward = jnp.where(is_last, index % 2 == 0, index < micro)
+        m = jnp.where(is_last, index // 2, index % micro)
+        pl.when(forward)(lambda: forward_step(m))
+        pl.when(not_last & (index == micro))(turn_round)
+        pl.when(jnp.logical_not(forward))(lambda: backward_step(m))
         return carry
 
-    lax.fori_loop(0, micro, backward_step, 0)
+    lax.fori_loop(0, 2 * micro, step, 0)
 
     def finish_hops():
         for m in range(micro):
@@ -605,30 +641,42 @@
             target[...] = (target[...].astype(F32) + k.prx[part, chip].astype(F32)).astype(BF16)
         chain(0, part)
 
+    def nearby(index):
+        low = z + (index % 2) * (1 - 2 * (z % 2))
+        return low + (index // 2) * (2 - 4 * ((low // 2) % 2))
+
+    start = width * z
+
+    @pl.when(not_last & (sec > 0))
+    def _():
+        for early in range(micro - 1):
+            relay(*errs, early, 1)
+
     @pl.when(not_last)
     def _():
         relay(*errs, micro - 1, 1)
-        for m in range(micro):
-            relay(*errs, m, 2)
-
-    pl.when(is_last)(relay_acts)
+
+    @pl.when(not_last & (sec > 0))
+    def _():
+        for early in range(micro - 1):
+            relay(*errs, early, 2)
+
+    pl.when(is_last)(lambda: relay_acts(1))
+    pl.when(sec >= count - 2)(lambda: relay_acts(*range(2, chips - 1)))
+    mlp_weight_grads(k, z, start, True)
+    chain(1, 0)
+
+    @pl.when(not_last)
+    def _():
+        relay(*errs, micro - 1, 2)
+
+    mlp_weight_grads(k, nearby(1), start, False)
+    chain(1, 1)
+    mlp_weight_grads(k, nearby(2), start, False)
+    chain(1, 2)
     for m in range(micro):
         relay(*acts, m, chips - 1)
-
-    def nearby(index):
-        low = z + (index % 2) * (1 - 2 * (z % 2))
-        return low + (index // 2) * (2 - 4 * ((low // 2) % 2))
-
-    start = width * z
-    mlp_weight_grads(k, z, start, True)
-    chain(1, 0)
-    chain(2, 0)
-    mlp_weight_grads(k, nearby(1), start, False)
-    chain(1, 1)
-    chain(2, 1)
-    for m in range(micro):
         relay(*errs, m, chips - 1)
-    mlp_weight_grads(k, nearby(2), start, False)
     mlp_weight_grads(k, nearby(3), start, False)
 
     per_core = hidden // peers
@@ -672,9 +720,10 @@
     final.start()
     finals.append(final)
 
-    for part in range(2, 4):
-        chain(1, part)
+    for part in range(3):
         chain(2, part)
+    chain(1, 3)
+    chain(2, 3)
     for part in range(4):
         at = part_rows(part, 1 - core)
         k.pool[at, :] = part_ref(part, z, core)[...].astype(F32)
@@ -728,6 +777,38 @@
     for final in finals:
         final.wait()
     finish_hops()
+
+
+def deliver_kernel(count, *refs):
+    sources, targets, held = refs[:count], refs[count : 2 * count], refs[2 * count : 3 * count]
+    sems = refs[-1]
+    fetches = [
+        pltpu.make_async_copy(sources[i], held[i], sems.at[0, i]) for i in range(count)
+    ]
+    stores = [
+        pltpu.make_async_copy(held[i], targets[i], sems.at[1, i]) for i in range(count)
+    ]
+    for fetch in fetches:
+        fetch.start()
+    for fetch, store in zip(fetches, stores):
+        fetch.wait()
+        store.start()
+    for store in stores:
+        store.wait()
+
+
+def deliver(arrays):
+    anywhere = pl.BlockSpec(memory_space=pl.ANY)
+    count = len(arrays)
+    return pl.pallas_call(
+        partial(deliver_kernel, count),
+        out_shape=tuple(jax.ShapeDtypeStruct(a.shape, a.dtype) for a in arrays),
+        in_specs=[anywhere] * count,
+        out_specs=(anywhere,) * count,
+        scratch_shapes=[pltpu.VMEM(a.shape, a.dtype) for a in arrays]
+        + [pltpu.SemaphoreType.DMA((2, count))],
+        compiler_params=pltpu.CompilerParams(vmem_limit_bytes=62 << 20),
+    )(*arrays)
 
 
 def shards(patches, lengths, qkv_weight, out_weight, up_weight, down_weight, vectors, cotangent):
@@ -754,7 +835,7 @@
         ),
         in_specs=[
             anywhere,
-            pl.BlockSpec(memory_space=pltpu.SMEM),
+            anywhere,
             anywhere,
             anywhere,
             anywhere,
@@ -769,7 +850,7 @@
         ),
     )(
         patches[:, 0],
-        lengths,
+        lengths[:, 0],
         qkv_weight,
         out_weight,
         up_weight,
@@ -777,6 +858,8 @@
         vectors,
         cotangent[:, 0],
     )
+    if fused:
+        results = deliver(results)
     outputs, input_grads, *grads, vector_grad = results
     if fused:
         grads = [grad[None] for grad in grads]

time: 224 us -> 203 us (0.906)
  Pallas kernels: 213 us -> 202 us
  local copies, waits for them, and re-layouts: 9.68 us -> 0 us
    pallas_call x1, Pallas kernels: 213 us -> 197 us  [shards(): pl.pallas_call(partial(pipeline_kernel, tuple(plan), fused), out_shape=(j...]
    unnamed x20 -> x0, local copies, waits for them, and re-layouts: 9.68 us -> none
    pallas_call x0 -> x1, Pallas kernels: none -> 5.07 us  [deliver(): pl.pallas_call(partial(deliver_kernel, count), out_shape=tuple((jax.Shape...]
where the time goes in v3:
time: 203 us
  Pallas kernels  202 us (100%)
    pallas_call x1, Pallas kernels, shards(): pl.pallas_call(partial(pipeline_kernel, tuple(plan), fused), out_shape=(j...  197 us
    pallas_call x1, Pallas kernels, deliver(): pl.pallas_call(partial(deliver_kernel, count), out_shape=tuple((jax.Shape...  5.07 us

profile of v3, /device:TPU:0, one launch (start us, length us, event | category | flops | bytes accessed | tf_op | source)
XLA Modules:
  0.0 203.2 jit_solution(4230821341115800189)
XLA Ops:
  0.6 197.3 %shard_map.135 = (bf16[2,256,768]{2,1,0:T(8,128)(2,1)}, f32[2,256,768]{2,1,0:T(8,128)}, f32[96,2304]{1,0:T(8,128)}, f32[96,768]{1,0:T(8,128)}, f32[96,3072]{1,0:...) custom-call(bf16[2,256,768]{2,1,0:T(8,128)(2,1)} %bitcast.13, s32[2]{0:T(128)} %bitcast.15, ...), custom_call_target="tpu_custom_call" | custom-call | tf_op jit(solution)/shard_map/pallas_call | solution.py:825
  198.0 5.1 %shard_map.136 = (bf16[2,256,768]{2,1,0:T(8,128)(2,1)}, f32[2,256,768]{2,1,0:T(8,128)}, f32[96,2304]{1,0:T(8,128)}, f32[96,768]{1,0:T(8,128)}, f32[96,3072]{1,0:...) custom-call(bf16[2,256,768]{2,1,0:T(8,128)(2,1)} %get-tuple-element.21.refs_0_, ...), custom_call_target="tpu_custom_call" | custom-call | tf_op jit(solution)/shard_map/pallas_call | solution.py:803

commit v4 on v3

--- a/solution.py
+++ b/solution.py
@@ -72,11 +72,12 @@
         p=vm((micro, heads, rows, rows), BF16),
         wide=vm((rows, hidden), BF16),
         gp=vm((micro, rows, hidden), BF16),
+        du=vm((micro, rows, hidden), BF16),
         dp=vm((micro, rows, 3 * width), BF16),
         do=vm((rows, width), BF16),
         doo=vm((rows, width), BF16),
         rest=vm((rows, width), BF16),
-        pool=vm((2 * width, width), F32),
+        pool=vm((chips * UP_ROWS + width, width) if fused else (2 * width, width), F32),
         ig=vm((micro, rows, width), F32),
         lens=pltpu.SMEM((micro,), jnp.int32),
         lsem=dma((1,)),
@@ -108,15 +109,12 @@
             vrx=vm((peers, 1, (8 * width + hidden) // peers), F32),
             vsend=dma((peers,)),
             vrecv=dma((peers,)),
-            upx=vm((chips, 2, share, width), BF16),
+            upx=vm((chips, share, width), BF16),
             uprx=vm((chips, share, width), BF16),
             upsem=dma((2,)),
             dnx=vm((hidden // peers, width), BF16),
             dnrx=vm((hidden // peers, width), BF16),
             dnsem=dma((2,)),
-            uax=vm((chips, share, width), BF16),
-            uasend=dma((chips,)),
-            uarecv=dma((chips,)),
             turn=pltpu.SemaphoreType.REGULAR,
         )
     return plan
@@ -133,6 +131,7 @@
 
 
 RL, OF, MID = 0, 2, 4
+UP_ROWS = 256
 
 
 def forward_attention(k, m, z, key_bias):
@@ -201,9 +200,9 @@
         grad_up = (
             nt(grad, k.wdown[c : c + 256, :]) * k.gp[m, :, c : c + 256].astype(F32)
         ).astype(BF16)
-        k.wide[:, c : c + 256] = grad_up
+        k.du[m, :, c : c + 256] = grad_up
         add_sums(gvec, 8 * width + c, grad_up.astype(F32))
-    grad_two = nt(k.wide[...], k.wup[...])
+    grad_two = nt(k.du[m], k.wup[...])
     unit = k.n2[m].astype(F32)
     add_sums(gvec, 5 * width, grad_two * unit)
     add_sums(gvec, 6 * width, grad_two)
@@ -216,13 +215,15 @@
     add_sums(gvec, 4 * width, branch.astype(F32))
 
 
-def backward_attention(k, gvec, m):
-    rows, width = k.x.shape[1:]
-    vec = k.vec
+def backward_out(k, m):
     k.do[...] = (nt(k.x[m], k.wout[...]) * k.pool[pool_rows(k, RL, m), :]).astype(BF16)
     product = k.do[...].astype(F32) * k.pool[pool_rows(k, OF, m), :]
     k.doo[...] = product.astype(BF16)
     k.rest[...] = (product - k.doo[...].astype(F32)).astype(BF16)
+
+
+def backward_heads(k, gvec, m):
+    rows, width = k.x.shape[1:]
     low, high, first = pair_masks()
     minus = jnp.full((rows, 128), -1.0, BF16)
     scale = HEAD_DIM**-0.5
@@ -249,18 +250,28 @@
         k.dp[m, :, 2 * width + c : 2 * width + c + 128] = grad_v
         add_sums(gvec, 2 * width + c, grad_q.astype(F32))
         add_sums(gvec, 3 * width + c, grad_v.astype(F32))
+
+
+def backward_qkv(k, gvec, m):
+    width = k.x.shape[2]
     grad_one = nt(k.dp[m], k.wqkv[...])
     unit = k.n1[m].astype(F32)
     add_sums(gvec, 0, grad_one * unit)
     add_sums(gvec, width, grad_one)
     grad_in = k.pool[pool_rows(k, MID), :] + norm_back(
-        grad_one * (1.0 + vec[:, :width]), unit, k.r1[m, :, :1]
+        grad_one * (1.0 + k.vec[:, :width]), unit, k.r1[m, :, :1]
     )
     k.ig[m] = grad_in
     k.y[m] = grad_in.astype(BF16)
 
 
-def attention_weight_grads(k, after_chunk):
+def out_weight_grad(k):
+    micro, rows, width = k.x.shape
+    both = micro * rows
+    k.wout[...] = tn(k.o[...].reshape(both, width), k.x[...].reshape(both, width)).astype(BF16)
+
+
+def qkv_weight_grads(k, after_chunk):
     micro, rows, width = k.x.shape
     both = micro * rows
     normed = k.a1[...].reshape(both, width)
@@ -268,8 +279,6 @@
         grads = k.dp[:, :, part * width : (part + 1) * width].reshape(both, width)
         k.wqkv[:, part * width : (part + 1) * width] = tn(normed, grads).astype(BF16)
         after_chunk(part)
-    k.wout[...] = tn(k.o[...].reshape(both, width), k.x[...].reshape(both, width)).astype(BF16)
-    after_chunk(3)
 
 
 def mlp_weight_grads(k, origin, start, fresh):
@@ -292,6 +301,40 @@
             k.pool[width + c : width + c + 256, :] += down
 
 
+def own_weight_grads(k, z, rows_at, down_at):
+    micro, rows, width = k.x.shape
+    both = micro * rows
+    normed = k.a2[:, z].reshape(both, width)
+    picked = k.a2[:, z, :, rows_at].reshape(both, UP_ROWS)
+    grad = k.e[:, z].reshape(both, width)
+    for c in range(0, width, 256):
+        at = pl.ds(pl.multiple_of(z * width + c, 256), 256)
+        bias = k.vec[:, pl.ds(pl.multiple_of(8 * width + z * width + c, 256), 256)]
+        value, _ = gelu_pair(nn(normed, k.wup[:, at]) + bias)
+        k.pool[down_at + c : down_at + c + 256, :] = tn(value.astype(BF16), grad)
+    for c in range(0, k.wup.shape[1], width):
+        at = c // width * UP_ROWS
+        grads = k.du[:, :, c : c + width].reshape(both, width)
+        k.pool[at : at + UP_ROWS, :] = tn(picked, grads)
+
+
+def slice_weight_grads(k, origin, piece, rows_at, down_at):
+    micro, rows, width = k.x.shape
+    both = micro * rows
+    normed = k.a2[:, origin].reshape(both, width)
+    picked = k.a2[:, origin, :, rows_at].reshape(both, UP_ROWS)
+    grad = k.e[:, origin].reshape(both, width)
+    up_at = pl.ds(pl.multiple_of(piece * UP_ROWS, UP_ROWS), UP_ROWS)
+    for c in range(0, width, 256):
+        at = pl.ds(pl.multiple_of(piece * width + c, 256), 256)
+        bias = k.vec[:, pl.ds(pl.multiple_of(8 * width + piece * width + c, 256), 256)]
+        value, slope = gelu_pair(nn(normed, k.wup[:, at]) + bias)
+        grad_up = (nt(grad, k.wdown[at, :]) * slope).astype(BF16)
+        k.pool[up_at, c : c + 256] += tn(picked, grad_up)
+        if down_at is not None:
+            k.pool[down_at + c : down_at + c + 256, :] += tn(value.astype(BF16), grad)
+
+
 def pipeline_kernel(scratch_names, fused, *refs):
     k = Refs(INPUTS + RESULTS + scratch_names, refs)
     sec = lax.axis_index("section")
@@ -449,6 +492,27 @@
                 for m in range(micro):
                     relay(*errs, m, distance)
 
+    sibling = me + 1 - 2 * core
+
+    def part_rows(chip, parity):
+        return pl.ds(pl.multiple_of(share * (2 * chip + parity), share), share)
+
+    def part_ref(part, chip, parity):
+        if part < 3:
+            return k.wqkv.at[part_rows(chip, parity), pl.ds(part * width, width)]
+        return k.wout.at[part_rows(chip, parity), :]
+
+    def pair_copy(part, chip):
+        return to_peer(
+            part_ref(part, chip, 1 - core), k.prx.at[part, chip],
+            k.pxsend.at[part, chip], k.pxrecv.at[part, chip], sibling,
+        )
+
+    def send_pair(part):
+        for chip in range(chips):
+            pair_copy(part, chip).start()
+
+    ends_first = is_first & not_last if fused else False
     waits_turn = is_first & (core == 1) & not_last
 
     def forward_step(m):
@@ -499,13 +563,18 @@
                 share_own(*errs, m)
 
         backward_mlp(k, gvec, m, z)
+        backward_out(k, m)
         if fused:
-            @pl.when(is_first & not_last & (m == micro - 1))
-            def _():
+            @pl.when(ends_first & (m == micro - 1))
+            def _():
+                out_weight_grad(k)
+                send_pair(3)
                 for early in range(micro - 1):
                     relay(*errs, early, 2)
 
-        backward_attention(k, gvec, m)
+        backward_heads(k, gvec, m)
+
+        backward_qkv(k, gvec, m)
 
         @pl.when(sec > 0)
         def _():
@@ -513,7 +582,7 @@
 
         in_copy(m).start()
         if fused:
-            @pl.when(is_first & not_last & (m < micro - 1))
+            @pl.when(ends_first & (m < micro - 1))
             def _():
                 relay(*errs, m, 1)
 
@@ -558,7 +627,8 @@
                 e_send(m).wait_send()
 
     if not fused:
-        attention_weight_grads(k, lambda part: None)
+        out_weight_grad(k)
+        qkv_weight_grads(k, lambda part: None)
         for c in range(0, hidden, width):
             mlp_weight_grads(k, 0, c, True)
             k.wup[:, c : c + width] = k.pool[:width, :].astype(BF16)
@@ -576,27 +646,12 @@
         finish_hops()
         return
 
-    sibling = me + 1 - 2 * core
-
-    def part_rows(chip, parity):
-        return pl.ds(pl.multiple_of(share * (2 * chip + parity), share), share)
-
-    def part_ref(part, chip, parity):
-        if part < 3:
-            return k.wqkv.at[part_rows(chip, parity), pl.ds(part * width, width)]
-        return k.wout.at[part_rows(chip, parity), :]
-
-    def pair_copy(part, chip):
-        return to_peer(
-            part_ref(part, chip, 1 - core), k.prx.at[part, chip],
-            k.pxsend.at[part, chip], k.pxrecv.at[part, chip], sibling,
-        )
-
-    def send_pair(part):
-        for chip in range(chips):
-            pair_copy(part, chip).start()
-
-    attention_weight_grads(k, send_pair)
+    @pl.when(jnp.logical_not(ends_first))
+    def _():
+        out_weight_grad(k)
+        send_pair(3)
+
+    qkv_weight_grads(k, send_pair)
 
     length = gvec.shape[1] // peers
 
@@ -619,14 +674,14 @@
             me + 2 if up else me - 2,
         )
 
-    def chain(stage, part):
+    def chain(stage, place, parts=range(4)):
         for up in (True, False):
             @pl.when((z if up else chips - 1 - z) == stage)
             def _():
-                for place in range(chips - 1, stage, -1):
+                chip = place if up else chips - 1 - place
+                for part in parts:
                     if stage > 0:
                         chain_copy(up, part, place).wait_recv()
-                        chip = place if up else chips - 1 - place
                         target = part_ref(part, chip, core)
                         target[...] = (
                             target[...].astype(F32)
@@ -634,125 +689,127 @@
                         ).astype(BF16)
                     chain_copy(up, part, place).start()
 
-    for part in range(4):
+    for part in (3, 0, 1, 2):
         for chip in range(chips):
             pair_copy(part, chip).wait()
             target = part_ref(part, chip, core)
             target[...] = (target[...].astype(F32) + k.prx[part, chip].astype(F32)).astype(BF16)
-        chain(0, part)
-
+        chain(0, chips - 1, (part,))
+
+    def follow(place):
+        for up in (True, False):
+            @pl.when((z if up else chips - 1 - z) == 0)
+            def _():
+                for part in range(4):
+                    chain_copy(up, part, place + 1).wait_send()
+                for part in range(4):
+                    chain_copy(up, part, place).start()
+
+    @pl.when(not_last & (sec > 0))
+    def _():
+        for early in range(micro - 1):
+            relay(*errs, early, 1)
+
+    @pl.when(not_last)
+    def _():
+        relay(*errs, micro - 1, 1)
+
+    @pl.when(not_last & (sec > 0))
+    def _():
+        for early in range(micro - 1):
+            relay(*errs, early, 2)
+
+    pl.when(is_last)(lambda: relay_acts(1))
+    pl.when(sec >= count - 2)(lambda: relay_acts(*range(2, chips - 1)))
     def nearby(index):
         low = z + (index % 2) * (1 - 2 * (z % 2))
         return low + (index // 2) * (2 - 4 * ((low // 2) % 2))
 
-    start = width * z
-
-    @pl.when(not_last & (sec > 0))
-    def _():
-        for early in range(micro - 1):
-            relay(*errs, early, 1)
-
-    @pl.when(not_last)
-    def _():
-        relay(*errs, micro - 1, 1)
-
-    @pl.when(not_last & (sec > 0))
-    def _():
-        for early in range(micro - 1):
-            relay(*errs, early, 2)
-
-    pl.when(is_last)(lambda: relay_acts(1))
-    pl.when(sec >= count - 2)(lambda: relay_acts(*range(2, chips - 1)))
-    mlp_weight_grads(k, z, start, True)
-    chain(1, 0)
-
-    @pl.when(not_last)
+    rows_at = pl.ds(pl.multiple_of(128 * ((3 * z) // 2), 128), UP_ROWS)
+    down_base = chips * UP_ROWS
+
+    def batch(origin):
+        slice_weight_grads(k, origin, z, rows_at, down_base)
+
+        def other(step, carry):
+            slice_weight_grads(k, origin, (z + step) % chips, rows_at, None)
+            return carry
+
+        lax.fori_loop(1, chips, other, 0)
+
+    inner = (z > 0) & (z < chips - 1)
+
+    @pl.when(not_last & inner)
     def _():
         relay(*errs, micro - 1, 2)
 
-    mlp_weight_grads(k, nearby(1), start, False)
-    chain(1, 1)
-    mlp_weight_grads(k, nearby(2), start, False)
+    own_weight_grads(k, z, rows_at, down_base)
+    follow(2)
+    chain(1, 3, (3, 0, 1, 2))
+
+    @pl.when(not_last & jnp.logical_not(inner))
+    def _():
+        relay(*errs, micro - 1, 2)
+
+    batch(nearby(1))
     chain(1, 2)
+    batch(nearby(2))
+    follow(1)
+    chain(2, 3, (3, 0, 1, 2))
     for m in range(micro):
         relay(*acts, m, chips - 1)
         relay(*errs, m, chips - 1)
-    mlp_weight_grads(k, nearby(3), start, False)
+    batch(nearby(3))
 
     per_core = hidden // peers
-    k.dnx[...] = k.pool[pl.ds(pl.multiple_of(width + per_core * (1 - core), per_core), per_core), :].astype(BF16)
+
+    def down_rows(parity):
+        return pl.ds(pl.multiple_of(down_base + per_core * parity, 128), per_core)
+
+    def up_rows(piece, parity):
+        first_row = UP_ROWS * piece + (UP_ROWS - 2 * share) * (z % 2) + share * parity
+        return pl.ds(pl.multiple_of(first_row, 32), share)
+
+    for piece in range(chips):
+        k.upx[piece] = k.pool[up_rows(piece, 1 - core), :].astype(BF16)
+    up_pair = to_peer(k.upx, k.uprx, k.upsem.at[0], k.upsem.at[1], sibling)
+    up_pair.start()
+    k.dnx[...] = k.pool[down_rows(1 - core), :].astype(BF16)
     down_pair = to_peer(k.dnx, k.dnrx, k.dnsem.at[0], k.dnsem.at[1], sibling)
     down_pair.start()
-    for chip in range(chips):
-        for parity in range(2):
-            k.upx[chip, parity] = k.pool[
-                share * (2 * chip + parity) : share * (2 * chip + parity + 1), :
-            ].astype(BF16)
-    up_pair = to_peer(k.upx.at[:, 1 - core], k.uprx, k.upsem.at[0], k.upsem.at[1], sibling)
-    up_pair.start()
+    finals = []
     up_pair.wait()
-
-    def spread(chip):
-        return to_peer(
-            k.upx.at[chip, core], k.uax.at[z], k.uasend.at[chip], k.uarecv.at[z], 2 * chip + core
-        )
-
-    def gathered(chip):
-        return to_peer(
-            k.upx.at[chip, core], k.uax.at[chip], k.uasend.at[chip], k.uarecv.at[chip], 2 * chip + core
-        )
-
-    finals = []
-    for chip in range(chips):
-        at = part_rows(chip, core)
-        total = k.pool[at, :] + k.uprx[chip].astype(F32)
-        k.pool[at, :] = total
-        k.upx[chip, core] = total.astype(BF16)
-
-        @pl.when(z != chip)
-        def _():
-            spread(chip).start()
-
+    for piece in range(chips):
+        at = up_rows(piece, core)
+        k.pool[at, :] += k.uprx[piece].astype(F32)
+        final = pltpu.make_async_copy(
+            k.pool.at[at], k.up_grad.at[:, pl.ds(piece * width, width)], k.gsem.at[5 + piece]
+        )
+        final.start()
+        finals.append(final)
     down_pair.wait()
-    down_at = pl.ds(pl.multiple_of(width + per_core * core, per_core), per_core)
-    k.pool[down_at, :] += k.dnrx[...].astype(F32)
-    final = pltpu.make_async_copy(k.pool.at[down_at], k.down_grad, k.gsem.at[0])
+    k.pool[down_rows(core), :] += k.dnrx[...].astype(F32)
+    final = pltpu.make_async_copy(k.pool.at[down_rows(core)], k.down_grad, k.gsem.at[0])
     final.start()
     finals.append(final)
-
-    for part in range(3):
-        chain(2, part)
-    chain(1, 3)
-    chain(2, 3)
+    finish_hops()
+
     for part in range(4):
-        at = part_rows(part, 1 - core)
-        k.pool[at, :] = part_ref(part, z, core)[...].astype(F32)
+        held = k.ig.at[part // 2, pl.ds(share * (part % 2), share)]
+        held[...] = part_ref(part, z, core)[...].astype(F32)
 
         @pl.when(z > 0)
         def _():
             chain_copy(True, part, z).wait_recv()
-            k.pool[at, :] += k.rsx[0, part, z - 1].astype(F32)
+            held[...] += k.rsx[0, part, z - 1].astype(F32)
 
         @pl.when(z < chips - 1)
         def _():
             chain_copy(False, part, chips - 1 - z).wait_recv()
-            k.pool[at, :] += k.rsx[1, part, chips - 2 - z].astype(F32)
+            held[...] += k.rsx[1, part, chips - 2 - z].astype(F32)
 
         target = k.qkv_grad.at[:, pl.ds(part * width, width)] if part < 3 else k.out_grad
-        final = pltpu.make_async_copy(k.pool.at[at], target, k.gsem.at[1 + part])
-        final.start()
-        finals.append(final)
-    for chip in range(chips):
-        at = part_rows(chip, core)
-
-        @pl.when(z != chip)
-        def _():
-            gathered(chip).wait_recv()
-            k.pool[at, :] = k.uax[chip].astype(F32)
-
-        final = pltpu.make_async_copy(
-            k.pool.at[at], k.up_grad.at[:, pl.ds(chip * width, width)], k.gsem.at[5 + chip]
-        )
+        final = pltpu.make_async_copy(held, target, k.gsem.at[1 + part])
         final.start()
         finals.append(final)
     own = gvec[:, pl.ds(pl.multiple_of(me * length, 128), length)]
@@ -767,16 +824,13 @@
     for part in range(4):
         for up in (True, False):
             for place in range(1, chips):
-                @pl.when((z if up else chips - 1 - z) < place)
+                position = z if up else chips - 1 - z
+
+                @pl.when((position < place) & ((position > 0) | (place == 1)))
                 def _():
                     chain_copy(up, part, place).wait_send()
-    for chip in range(chips):
-        @pl.when(z != chip)
-        def _():
-            spread(chip).wait_send()
     for final in finals:
         final.wait()
-    finish_hops()
 
 
 def deliver_kernel(count, *refs):
@@ -815,7 +869,7 @@
     micro, _, rows, width = patches.shape
     hidden = up_weight.shape[2]
     peers = lax.axis_size("dp")
-    fused = peers == 8 and hidden == peers // 2 * width
+    fused = peers == 8 and hidden == peers // 2 * width and 4 * (width // peers) == 3 * 128
     chips = peers // 2 if fused else 1
     plan = scratch_plan(micro, rows, width, hidden, chips, peers, fused)
     anywhere = pl.BlockSpec(memory_space=pl.ANY)

time: 203 us -> 192 us (0.946)
  Pallas kernels: 202 us -> 191 us
    pallas_call x1, Pallas kernels: 197 us -> 186 us  [shards(): pl.pallas_call(partial(pipeline_kernel, tuple(plan), fused), out_shape=(j...]
where the time goes in v4:
time: 192 us
  Pallas kernels  191 us (99%)
    pallas_call x1, Pallas kernels, shards(): pl.pallas_call(partial(pipeline_kernel, tuple(plan), fused), out_shape=(j...  186 us
    pallas_call x1, Pallas kernels, deliver(): pl.pallas_call(partial(deliver_kernel, count), out_shape=tuple((jax.Shape...  5.07 us

profile of v4, /device:TPU:0, one launch (start us, length us, event | category | flops | bytes accessed | tf_op | source)
XLA Modules:
  0.0 191.8 jit_solution(13889508493589169561)
XLA Ops:
  0.6 185.9 %shard_map.135 = (bf16[2,256,768]{2,1,0:T(8,128)(2,1)}, f32[2,256,768]{2,1,0:T(8,128)}, f32[96,2304]{1,0:T(8,128)}, f32[96,768]{1,0:T(8,128)}, f32[96,3072]{1,0:...) custom-call(bf16[2,256,768]{2,1,0:T(8,128)(2,1)} %bitcast.13, s32[2]{0:T(128)} %bitcast.15, ...), custom_call_target="tpu_custom_call" | custom-call | tf_op jit(solution)/shard_map/pallas_call | solution.py:879
  186.6 5.1 %shard_map.136 = (bf16[2,256,768]{2,1,0:T(8,128)(2,1)}, f32[2,256,768]{2,1,0:T(8,128)}, f32[96,2304]{1,0:T(8,128)}, f32[96,768]{1,0:T(8,128)}, f32[96,3072]{1,0:...) custom-call(bf16[2,256,768]{2,1,0:T(8,128)(2,1)} %get-tuple-element.21.refs_0_, ...), custom_call_target="tpu_custom_call" | custom-call | tf_op jit(solution)/shard_map/pallas_call | solution.py:857

commit v5 on v4

--- a/solution.py
+++ b/solution.py
@@ -728,10 +728,12 @@
     rows_at = pl.ds(pl.multiple_of(128 * ((3 * z) // 2), 128), UP_ROWS)
     down_base = chips * UP_ROWS
 
-    def batch(origin):
+    def batch(origin, hooks=()):
         slice_weight_grads(k, origin, z, rows_at, down_base)
 
         def other(step, carry):
+            for at, hook in hooks:
+                pl.when(step == at)(hook)
             slice_weight_grads(k, origin, (z + step) % chips, rows_at, None)
             return carry
 
@@ -739,26 +741,27 @@
 
     inner = (z > 0) & (z < chips - 1)
 
-    @pl.when(not_last & inner)
-    def _():
-        relay(*errs, micro - 1, 2)
-
+    def relay_inner():
+        @pl.when(not_last & inner)
+        def _():
+            relay(*errs, micro - 1, 2)
+
+    outward = (3, 0, 1, 2)
     own_weight_grads(k, z, rows_at, down_base)
-    follow(2)
-    chain(1, 3, (3, 0, 1, 2))
+    batch(nearby(1), ((2, relay_inner), (2, lambda: follow(2))))
+    chain(1, 3, outward)
 
     @pl.when(not_last & jnp.logical_not(inner))
     def _():
         relay(*errs, micro - 1, 2)
 
-    batch(nearby(1))
-    chain(1, 2)
     batch(nearby(2))
     follow(1)
-    chain(2, 3, (3, 0, 1, 2))
+    chain(1, 2)
     for m in range(micro):
         relay(*acts, m, chips - 1)
         relay(*errs, m, chips - 1)
+    chain(2, 3, outward)
     batch(nearby(3))
 
     per_core = hidden // peers

time: 192 us -> 185 us (0.964)
  Pallas kernels: 191 us -> 183 us
    pallas_call x1, Pallas kernels: 186 us -> 178 us  [shards(): pl.pallas_call(partial(pipeline_kernel, tuple(plan), fused), out_shape=(j...]
where the time goes in v5:
time: 185 us; the launch traced here: 184 us
  Pallas kernels  183 us (99%)
    pallas_call x1, Pallas kernels, shards(): pl.pallas_call(partial(pipeline_kernel, tuple(plan), fused), out_shape=(j...  178 us
    pallas_call x1, Pallas kernels, deliver(): pl.pallas_call(partial(deliver_kernel, count), out_shape=tuple((jax.Shape...  5.07 us

profile of v5, /device:TPU:0, one launch (start us, length us, event | category | flops | bytes accessed | tf_op | source)
XLA Modules:
  0.0 183.6 jit_solution(13899545607522059308)
XLA Ops:
  0.6 177.7 %shard_map.135 = (bf16[2,256,768]{2,1,0:T(8,128)(2,1)}, f32[2,256,768]{2,1,0:T(8,128)}, f32[96,2304]{1,0:T(8,128)}, f32[96,768]{1,0:T(8,128)}, f32[96,3072]{1,0:...) custom-call(bf16[2,256,768]{2,1,0:T(8,128)(2,1)} %bitcast.13, s32[2]{0:T(128)} %bitcast.15, ...), custom_call_target="tpu_custom_call" | custom-call | tf_op jit(solution)/shard_map/pallas_call | solution.py:882
  178.4 5.1 %shard_map.136 = (bf16[2,256,768]{2,1,0:T(8,128)(2,1)}, f32[2,256,768]{2,1,0:T(8,128)}, f32[96,2304]{1,0:T(8,128)}, f32[96,768]{1,0:T(8,128)}, f32[96,3072]{1,0:...) custom-call(bf16[2,256,768]{2,1,0:T(8,128)(2,1)} %get-tuple-element.21.refs_0_, ...), custom_call_target="tpu_custom_call" | custom-call | tf_op jit(solution)/shard_map/pallas_call | solution.py:860
